TPU v7x, 32 devices: a whole 2x2x4 slice. The times are simulated.
32 devices in a mesh: ctx: 16 (over z, y, x), heads: 2 (over core).
Axes of the slice: x: 2, y: 2, z: 4, core: 2. Of those that a mesh axis runs over, the one named last changes fastest.
Arguments:
- resid_in: bfloat16 [2048, 5376], P('ctx', 'heads'), may hold values from -6 to 6
- first_layer_queries: bfloat16 [2048, 4096], P('ctx', 'heads'), may hold values from -270 to 270
- first_layer_keys: bfloat16 [2048, 2048], P('ctx', 'heads'), may hold values from -7 to 7
- first_layer_values: bfloat16 [2048, 2048], P('ctx', 'heads'), may hold values from -6 to 6
- out_one: bfloat16 [4096, 5376], P('heads'), may hold values from -6 to 6
- post_gain: float32 [5376], replicated, may hold values from 0.1 to 1.9
- pre_gain: float32 [5376], replicated, may hold values from 0.1 to 1.9
- proj_query: bfloat16 [5376, 4096], P('ctx', 'heads'), may hold values from -30 to 30
- key_projection: bfloat16 [5376, 2048], P('ctx', 'heads'), may hold values from -1 to 1
- value_projection: bfloat16 [5376, 2048], P('ctx', 'heads'), may hold values from -0.078125 to 0.078125
- window: int32 [32], P('heads'), may hold values from 512 to 1024, as said below
- positions: int32 [2048], replicated, may hold values from 0 to 1023, as said below
Outputs:
- resid_out: bfloat16 [2048, 5376], P('ctx', 'heads')
- attended: bfloat16 [2048, 4096], P('ctx', 'heads')
Inputs may be any that keep to these rules, and one draw needn't show every extreme that they name: Each query head's window counts back from and includes its own token; some head's window is exactly 1024. `positions`: tokens form three packed documents: a position is 0 at a document's first token and one more than the previous token's otherwise; one document has exactly 1024 tokens and none has more.
All inputs are finite; a program needn't handle non-finite values.
Results may differ from a plain program's by a relative error of at most 0.03.
Values may be sent and summed in bfloat16 or wider, within the bound.
A program may use at most 128 MiB of HBM per device.

v0:
```python
from functools import partial

import jax
import jax.numpy as jnp
from jax import lax
from jax.sharding import PartitionSpec as P

MODEL_WIDTH = 5376
HEAD_SIZE = 128
LONGEST_WINDOW = 1024


SCALE = 168.0 ** (-0.5)
EPS = 1e-06
THETA = 1000000.0
POSITION_FACTOR = 0.125


def shifted(value, axis, steps):
    count = lax.axis_size(axis)
    leading, last = (max(0, -steps), min(count, count - steps))
    return lax.ppermute(value, axis, [(source, source + steps) for source in range(leading, last)])


def from_partner(block, axis, bit):
    count = lax.axis_size(axis)
    route = []
    for low in range(count):
        high = low | 1 << bit
        if high != low and high < count:
            route += [(low, high), (high, low)]
    return lax.ppermute(block, axis, route)


def apply_rotary(values, pos_rows, factor):
    half_dim = values.shape[-1] // 2
    speeds = THETA ** (-(jnp.arange(half_dim, dtype=jnp.float32) * 2.0 / values.shape[-1]))
    angles = (pos_rows.astype(jnp.float32) * factor)[:, None] * speeds[None, :]
    cosine = jnp.cos(angles)[:, None, :]
    sine_part = jnp.sin(angles)[:, None, :]
    front_half = values[..., :half_dim]
    back_half = values[..., half_dim:]
    return jnp.concatenate(
        [front_half * cosine - back_half * sine_part, back_half * cosine + front_half * sine_part],
        axis=-1,
    )


def lookup(position_table, tokens):
    return jnp.take(position_table, jnp.clip(tokens, 0, position_table.shape[0] - 1))


def zig_token(row_ids, tok_dev):
    half_rows = tok_dev // 2
    device_of = row_ids // tok_dev
    local_row = row_ids % tok_dev
    last_pair = 2 * lax.axis_size("ctx") - 1
    return jnp.where(
        local_row < half_rows,
        2 * device_of * half_rows + local_row,
        (last_pair - 2 * device_of) * half_rows + local_row - half_rows,
    )


def masked_attention(
    query_row_block,
    key_row_block,
    value_row_block,
    query_tok,
    key_tok,
    query_pos,
    key_pos,
    window_limits,
):
    scores = (
        jnp.einsum(
            "qagd,kad->qagk", query_row_block, key_row_block, preferred_element_type=jnp.float32
        )
        * SCALE
    )
    distance = query_tok[:, None] - key_tok[None, :]
    base_ok = (
        (distance >= 0)
        & (key_tok[None, :] >= 0)
        & (query_pos[:, None] - key_pos[None, :] == distance)
    )
    visible = base_ok[:, None, None, :] & (
        distance[:, None, None, :] < window_limits[None, :, :, None]
    )
    row_peak = jnp.max(jnp.where(visible, scores, -1e30), axis=-1, keepdims=True)
    lifted = jnp.where(visible, jnp.exp(scores - row_peak), 0.0)
    row_total = jnp.sum(lifted, axis=-1)
    mixed = jnp.einsum(
        "qagk,kad->qagd",
        lifted.astype(jnp.bfloat16),
        value_row_block,
        preferred_element_type=jnp.float32,
    )
    return (mixed / row_total[..., None]).astype(jnp.bfloat16)


def mirror(rows_block, mover):
    half_rows = rows_block.shape[0] // 2
    travel = rows_block[half_rows:]
    bit_count = lax.axis_size("ctx").bit_length() - 1
    for bit_index in range(bit_count):
        travel = mover(travel, bit_index)
    return jnp.concatenate([rows_block[:half_rows], travel], axis=0)


def project(residual_rows, pre_gain, proj_query, key_projection, value_projection, row_pos):
    row_count = residual_rows.shape[0]
    widened = residual_rows.astype(jnp.float32)
    normalized_rows = (
        pre_gain[None, :]
        * widened
        * lax.rsqrt(jnp.mean(widened * widened, axis=1, keepdims=True) + EPS)
    ).astype(jnp.bfloat16)
    query_heads = proj_query.shape[1] // HEAD_SIZE
    pair_heads = key_projection.shape[1] // HEAD_SIZE
    second_layer_query = (
        apply_rotary(
            jnp.dot(
                normalized_rows,
                lax.all_gather(proj_query, "ctx", axis=0, tiled=True),
                preferred_element_type=jnp.float32,
            ).reshape(row_count, query_heads, HEAD_SIZE),
            row_pos,
            POSITION_FACTOR,
        )
        .astype(jnp.bfloat16)
        .reshape(row_count, query_heads * HEAD_SIZE)
    )
    second_layer_key = (
        apply_rotary(
            jnp.dot(
                normalized_rows,
                lax.all_gather(key_projection, "ctx", axis=0, tiled=True),
                preferred_element_type=jnp.float32,
            ).reshape(row_count, pair_heads, HEAD_SIZE),
            row_pos,
            POSITION_FACTOR,
        )
        .astype(jnp.bfloat16)
        .reshape(row_count, pair_heads * HEAD_SIZE)
    )
    second_layer_value = jnp.dot(
        normalized_rows,
        lax.all_gather(value_projection, "ctx", axis=0, tiled=True),
        preferred_element_type=jnp.float32,
    ).astype(jnp.bfloat16)
    return (second_layer_query, second_layer_key, second_layer_value)


def attend_block(
    state, query_row_block, key_block, value_block, query_tok, query_pos, block_tok, block_pos
):
    row_peak, row_total, weighted = state
    scores = (
        jnp.einsum("qagd,kad->qagk", query_row_block, key_block, preferred_element_type=jnp.float32)
        * SCALE
    )
    distance = query_tok[:, None] - block_tok[None, :]
    visible = (distance >= 0) & (query_pos[:, None] - block_pos[None, :] == distance)
    visible = visible[:, None, None, :]
    new_peak = jnp.maximum(row_peak, jnp.max(jnp.where(visible, scores, -1e30), axis=-1))
    lifted = jnp.where(visible, jnp.exp(scores - new_peak[..., None]), 0.0)
    shrink = jnp.exp(row_peak - new_peak)
    row_total = row_total * shrink + jnp.sum(lifted, axis=-1)
    weighted = weighted * shrink[..., None] + jnp.einsum(
        "qagk,kad->qagd",
        lifted.astype(jnp.bfloat16),
        value_block,
        preferred_element_type=jnp.float32,
    )
    return (new_peak, row_total, weighted)


def keep_state(state):
    return state


def shards(
    resid_in,
    first_layer_queries,
    first_layer_keys,
    first_layer_values,
    out_one,
    post_gain,
    pre_gain,
    proj_query,
    key_projection,
    value_projection,
    window,
    positions,
):
    tok_dev = resid_in.shape[0]
    col_width = resid_in.shape[1]
    ctx_place = lax.axis_index("ctx")
    head_place = lax.axis_index("heads")
    query_heads = first_layer_queries.shape[1] // HEAD_SIZE
    pair_heads = first_layer_keys.shape[1] // HEAD_SIZE
    group_length = query_heads // pair_heads
    window_limits = window.reshape(pair_heads, group_length)
    own_pairs = jnp.stack([first_layer_keys, first_layer_values])
    reach_count = LONGEST_WINDOW // tok_dev
    pieces = [own_pairs]
    for section in range(reach_count):
        pieces = [shifted(own_pairs, "ctx", section + 1)] + pieces
    extended = jnp.concatenate(pieces, axis=1)
    key_span = extended.shape[1]
    local_tok = ctx_place * tok_dev + jnp.arange(tok_dev, dtype=jnp.int32)
    key_tok = (ctx_place - reach_count) * tok_dev + jnp.arange(key_span, dtype=jnp.int32)
    attend_one = masked_attention(
        first_layer_queries.reshape(tok_dev, pair_heads, group_length, HEAD_SIZE),
        extended[0].reshape(key_span, pair_heads, HEAD_SIZE),
        extended[1].reshape(key_span, pair_heads, HEAD_SIZE),
        local_tok,
        key_tok,
        lookup(positions, local_tok),
        lookup(positions, key_tok),
        window_limits,
    )
    attend_one = attend_one.reshape(tok_dev, query_heads * HEAD_SIZE)
    partial_rows = jnp.dot(attend_one, out_one, preferred_element_type=jnp.float32)
    mirror_tok = zig_token(ctx_place * tok_dev + jnp.arange(tok_dev, dtype=jnp.int32), tok_dev)
    mirror_pos = lookup(positions, mirror_tok)
    shared = lax.psum_scatter(
        partial_rows.astype(jnp.bfloat16), "heads", scatter_dimension=1, tiled=True
    ).astype(jnp.float32)
    squares = lax.psum(jnp.sum(shared * shared, axis=1), "heads")
    post_scaled = shared * lax.rsqrt(squares[:, None] / MODEL_WIDTH + EPS)
    gain_slice = lax.dynamic_slice_in_dim(post_gain, head_place * col_width, col_width, 0)
    resid_out = (resid_in.astype(jnp.float32) + gain_slice[None, :] * post_scaled).astype(
        jnp.bfloat16
    )

    def move_resid(piece, bit_index):
        return from_partner(piece, "ctx", bit_index)

    relayed = mirror(resid_out, move_resid)
    residual_rows = lax.all_gather(relayed, "heads", axis=1, tiled=True)
    second_layer_query, second_layer_key, second_layer_value = project(
        residual_rows, pre_gain, proj_query, key_projection, value_projection, mirror_pos
    )
    half_rows = tok_dev // 2
    queries = second_layer_query.reshape(tok_dev, pair_heads, group_length, HEAD_SIZE)
    query_parts = (queries[:half_rows], queries[half_rows:])
    tok_parts = (mirror_tok[:half_rows], mirror_tok[half_rows:])
    pos_parts = (mirror_pos[:half_rows], mirror_pos[half_rows:])
    pair_two = jnp.stack([second_layer_key, second_layer_value])

    def empty_state():
        return (
            jnp.full((half_rows, pair_heads, group_length), -1e30, jnp.float32),
            jnp.zeros((half_rows, pair_heads, group_length), jnp.float32),
            jnp.zeros((half_rows, pair_heads, group_length, HEAD_SIZE), jnp.float32),
        )

    start_state = (empty_state(), empty_state())
    piece = lax.all_gather(pair_two, "ctx", axis=1, tiled=True)
    piece_rows = piece.shape[1]
    unit_rows = 2 * tok_dev
    unit_count = piece_rows // unit_rows

    def one_unit(index, state):
        offset = index * unit_rows
        unit_block = lax.dynamic_slice_in_dim(piece, offset, unit_rows, 1)
        current = list(state)
        for key_half in range(unit_rows // half_rows):
            key_block = unit_block[0, key_half * half_rows : (key_half + 1) * half_rows].reshape(
                half_rows, pair_heads, HEAD_SIZE
            )
            value_block = unit_block[1, key_half * half_rows : (key_half + 1) * half_rows].reshape(
                half_rows, pair_heads, HEAD_SIZE
            )
            key_row_block = offset + key_half * half_rows + jnp.arange(half_rows, dtype=jnp.int32)
            block_tok = zig_token(key_row_block, tok_dev)
            block_pos = lookup(positions, block_tok)
            earliest = jnp.min(block_tok)
            for query_half in range(2):
                work = partial(
                    attend_block,
                    query_row_block=query_parts[query_half],
                    key_block=key_block,
                    value_block=value_block,
                    query_tok=tok_parts[query_half],
                    query_pos=pos_parts[query_half],
                    block_tok=block_tok,
                    block_pos=block_pos,
                )
                needed = earliest <= tok_parts[query_half][half_rows - 1]
                current[query_half] = lax.cond(needed, work, keep_state, current[query_half])
        return tuple(current)

    final_state = lax.fori_loop(0, unit_count, one_unit, start_state)
    front = final_state[0][2] / final_state[0][1][..., None]
    back = final_state[1][2] / final_state[1][1][..., None]
    attended = (
        jnp.concatenate([front, back], axis=0)
        .astype(jnp.bfloat16)
        .reshape(tok_dev, query_heads * HEAD_SIZE)
    )
    return (resid_out, attended)


def solution(mesh):
    placed = (
        P("ctx", "heads"),
        P("ctx", "heads"),
        P("ctx", "heads"),
        P("ctx", "heads"),
        P("heads", None),
        P(),
        P(),
        P("ctx", "heads"),
        P("ctx", "heads"),
        P("ctx", "heads"),
        P("heads"),
        P(),
    )
    return jax.shard_map(
        shards,
        mesh=mesh,
        in_specs=placed,
        out_specs=(P("ctx", "heads"), P("ctx", "heads")),
        check_vma=False,
    )
```

profile of v0, /device:TPU:0, one launch (start us, length us, event | category | flops | bytes accessed | tf_op | source)
XLA Modules:
  0.0 1091.5 jit_solution(13048050869378220541)
XLA Ops:
  9.5 6.7 collective-permute-start
  16.3 6.2 collective-permute-start.1
  22.4 2.1 collective-permute-start.2
  29.0 6.5 gather_fusion.4
  35.7 1.9 fusion.130
  38.9 2.8 collective-permute-start.5
  42.8 15.3 %collective-permute-start.6 = (bf16[2,128,1024]{1,2,0:T(8,128)(2,1)S(1)}, bf16[2,128,1024]{1,2,0:T(8,128)(2,1)S(1)}, u32[]{:S(2)}, u32[]{:S(2)}) collective-permute-start(bf16[2,128,1024]{1,2,0:T(8,128)(2,1)S(1)} %pad_maximum_fusion.1), channel_id=1, source_target_pairs={{0,4},{2,6},{4,8},{6,10},{8,12},{10,14},{12,16},{14,18},{16,20},{1... | collective-permute-start | bytes 1572872 | tf_op jit(solution)/shard_map/ppermute | solution.py:22
  59.3 13.9 %collective-permute-start.7 = (bf16[2,128,1024]{1,2,0:T(8,128)(2,1)S(1)}, bf16[2,128,1024]{1,2,0:T(8,128)(2,1)S(1)}, u32[]{:S(2)}, u32[]{:S(2)}) collective-permute-start(bf16[2,128,1024]{1,2,0:T(8,128)(2,1)S(1)} %pad_maximum_fusion.1), channel_id=1, source_target_pairs={{0,2},{2,4},{4,6},{6,8},{8,10},{10,12},{12,14},{14,16},{16,18},{18... | collective-permute-start | bytes 1572872 | tf_op jit(solution)/shard_map/ppermute | solution.py:22
  75.0 8.7 collective-permute-done.7
  84.0 1.8 fusion.146
  85.8 11.1 %fusion.150 = (f32[128,8,2]{0,2,1:T(2,128)S(1)}, bf16[128,8,2,1152]{0,3,2,1:T(8,128)(2,1)}) fusion(s32[8,2]{1,0:T(8,128)S(1)} %lt.155, s32[128,1152]{0,1:T(8,128)S(1)} %broadcast_subtract_fusion, pred[128,1152]{0,1:T(8,128)(4,1)} %fusion.130, bf16[1152,8,128,1]{0,2,3,1:T(8,128)(2,1)} %bitcast.298, bf16[128,8,2,128]{3,2,1,0:T(2,128)(2,1)S(1)} %copy-done.5), kind=kOutput, calls=%fused_computation.303 | convolution fusion | flops 1233912960 | bytes 8347712 | tf_op jit(solution)/shard_map/sub | solution.py:91
  96.8 3.4 fusion.126
  100.3 10.4 convolution_convert_fusion
  112.5 92.3 %reduce-scatter.4.cloned.1.call-done = bf16[2688,128]{1,0:T(8,128)(2,1)} async-done(((bf16[5376,128]{1,0:T(8,128)(2,1)}), bf16[2688,128]{1,0:T(8,128)(2,1)}) %reduce-scatter.4.cloned.1.call-update) | async-done | bytes 688144
  206.4 2.5 psum.7
  209.3 1.8 collective-permute-start.8
  211.1 8.5 collective-permute-done.8
  219.6 1.8 collective-permute-start.9
  221.4 7.7 collective-permute-done.9
  229.0 1.7 collective-permute-start.10
  230.8 6.8 collective-permute-done.10
  237.6 2.7 collective-permute-start.11
  240.2 13.2 %collective-permute-done.11 = bf16[64,2688]{1,0:T(8,128)(2,1)S(1)} collective-permute-done((bf16[64,2688]{1,0:T(8,128)(2,1)S(1)}, bf16[64,2688]{1,0:T(8,128)(2,1)S(1)}, u32[]{:S(2)}, u32[]{:S(2)}) %collective-permute-start.11) | collective-permute-done | bytes 344096 | tf_op jit(solution)/shard_map/ppermute | solution.py:32
  258.0 7.1 all-gather.6.cloned.1.call-done
  266.8 139.9 %all-gather.8.cloned.1.call-done = bf16[5376,1024]{1,0:T(8,128)(2,1)} async-done(((bf16[336,1024]{1,0:T(8,128)(2,1)}), bf16[5376,1024]{1,0:T(8,128)(2,1)}) %all-gather.8.cloned.1.call-update) | async-done | bytes 11010064 | tf_op jit(solution)/shard_map/all_gather | solution.py:138
  406.7 6.2 convolution_bitcast_fusion.9
  413.6 131.5 %all-gather.10.cloned.1.call-done = bf16[5376,1024]{1,0:T(8,128)(2,1)} async-done(((bf16[336,1024]{1,0:T(8,128)(2,1)}), bf16[5376,1024]{1,0:T(8,128)(2,1)}) %all-gather.10.cloned.1.call-update) | async-done | bytes 11010064 | tf_op jit(solution)/shard_map/all_gather | solution.py:149
  545.1 5.9 fusion.129
  552.0 235.7 %all-gather.14.cloned.1.call-done = bf16[5376,2048]{1,0:T(8,128)(2,1)} async-done(((bf16[336,2048]{1,0:T(8,128)(2,1)}), bf16[5376,2048]{1,0:T(8,128)(2,1)}) %all-gather.14.cloned.1.call-update) | async-done | bytes 22020112 | tf_op jit(solution)/shard_map/all_gather | solution.py:125
  787.8 9.0 convolution_bitcast_fusion.8
  798.0 104.3 %all-gather.12.cloned.1.call-done = bf16[2,2048,1024]{2,1,0:T(8,128)(2,1)} async-done(((bf16[2,128,1024]{2,1,0:T(8,128)(2,1)}), bf16[2,2048,1024]{2,1,0:T(8,128)(2,1)}) %all-gather.12.cloned.1.call-update) | async-done | bytes 8388624 | tf_op jit(solution)/shard_map/all_gather | solution.py:261
  902.4 180.0 %while.26 = (s32[]{:T(128)}, f32[64,8,2]{0,2,1:T(2,128)S(1)}, f32[64,8,2]{0,2,1:T(2,128)S(1)}, f32[64,8,2,128]{3,0,2,1:T(8,128)S(1)}, f32[64,8,2]{0,2,1:T(2,128)...) while((s32[]{:T(128)}, f32[64,8,2]{0,2,1:T(2,128)S(1)}, ...), condition=%wide.region_43.46_spmd, body=%wide.region_6.45_spmd.sunk | while | flops 275468544 | bytes 23758332 | solution.py:296
  (630 shorter events, 162.0 us)
Async XLA Ops:
  7.2 21.8 %copy-start = (s32[2048]{0:T(1024)S(1)}, s32[2048]{0:T(1024)}, u32[]{:S(2)}) copy-start(s32[2048]{0:T(1024)} %param.45) | copy-start | bytes 24580
  7.2 197.6 %reduce-scatter.4.cloned.1.call-start = ((), (), s32[]{:S(2)}) async-start(), calls=%async_computation.6 | async-start | bytes 2064384
  9.5 29.4 %collective-permute-start = (bf16[2,128,1024]{1,2,0:T(8,128)(2,1)S(1)}, bf16[2,128,1024]{1,2,0:T(8,128)(2,1)}, u32[]{:S(2)}, u32[]{:S(2)}) collective-permute-start(bf16[2,128,1024]{1,2,0:T(8,128)(2,1)S(1)} %pad_maximum_fusion.1), channel_id=1, source_target_pairs={{0,16},{2,18},{4,20},{6,22},{8,24},{10,26},{12,28},{14,30},{1,17},... | collective-permute-start | bytes 1572872 | tf_op jit(solution)/shard_map/ppermute | solution.py:22
  16.3 26.5 %collective-permute-start.1 = (bf16[2,128,1024]{1,2,0:T(8,128)(2,1)S(1)}, bf16[2,128,1024]{1,2,0:T(8,128)(2,1)}, u32[]{:S(2)}, u32[]{:S(2)}) collective-permute-start(bf16[2,128,1024]{1,2,0:T(8,128)(2,1)S(1)} %pad_maximum_fusion.1), channel_id=1, source_target_pairs={{0,14},{2,16},{4,18},{6,20},{8,22},{10,24},{12,26},{14,28},{16,30}... | collective-permute-start | bytes 1572872 | tf_op jit(solution)/shard_map/ppermute | solution.py:22
  22.4 36.9 %collective-permute-start.2 = (bf16[2,128,1024]{1,2,0:T(8,128)(2,1)S(1)}, bf16[2,128,1024]{1,2,0:T(8,128)(2,1)}, u32[]{:S(2)}, u32[]{:S(2)}) collective-permute-start(bf16[2,128,1024]{1,2,0:T(8,128)(2,1)S(1)} %pad_maximum_fusion.1), channel_id=1, source_target_pairs={{0,12},{2,14},{4,16},{6,18},{8,20},{10,22},{12,24},{14,26},{16,28}... | collective-permute-start | bytes 1572872 | tf_op jit(solution)/shard_map/ppermute | solution.py:22
  24.5 49.9 %collective-permute-start.3 = (bf16[2,128,1024]{1,2,0:T(8,128)(2,1)S(1)}, bf16[2,128,1024]{1,2,0:T(8,128)(2,1)S(1)}, u32[]{:S(2)}, u32[]{:S(2)}) collective-permute-start(bf16[2,128,1024]{1,2,0:T(8,128)(2,1)S(1)} %pad_maximum_fusion.1), channel_id=1, source_target_pairs={{0,10},{2,12},{4,14},{6,16},{8,18},{10,20},{12,22},{14,24},{16,26}... | collective-permute-start | bytes 1572872 | tf_op jit(solution)/shard_map/ppermute | solution.py:22
  25.9 48.7 %collective-permute-start.4 = (bf16[2,128,1024]{1,2,0:T(8,128)(2,1)S(1)}, bf16[2,128,1024]{1,2,0:T(8,128)(2,1)S(1)}, u32[]{:S(2)}, u32[]{:S(2)}) collective-permute-start(bf16[2,128,1024]{1,2,0:T(8,128)(2,1)S(1)} %pad_maximum_fusion.1), channel_id=1, source_target_pairs={{0,8},{2,10},{4,12},{6,14},{8,16},{10,18},{12,20},{14,22},{16,24},... | collective-permute-start | bytes 1572872 | tf_op jit(solution)/shard_map/ppermute | solution.py:22
  28.9 8.8 copy-start.4
  29.0 9.9 copy-start.8
  38.9 35.8 %collective-permute-start.5 = (bf16[2,128,1024]{1,2,0:T(8,128)(2,1)S(1)}, bf16[2,128,1024]{1,2,0:T(8,128)(2,1)S(1)}, u32[]{:S(2)}, u32[]{:S(2)}) collective-permute-start(bf16[2,128,1024]{1,2,0:T(8,128)(2,1)S(1)} %pad_maximum_fusion.1), channel_id=1, source_target_pairs={{0,6},{2,8},{4,10},{6,12},{8,14},{10,16},{12,18},{14,20},{16,22},{... | collective-permute-start | bytes 1572872 | tf_op jit(solution)/shard_map/ppermute | solution.py:22
  42.8 32.0 %collective-permute-start.6 = (bf16[2,128,1024]{1,2,0:T(8,128)(2,1)S(1)}, bf16[2,128,1024]{1,2,0:T(8,128)(2,1)S(1)}, u32[]{:S(2)}, u32[]{:S(2)}) collective-permute-start(bf16[2,128,1024]{1,2,0:T(8,128)(2,1)S(1)} %pad_maximum_fusion.1), channel_id=1, source_target_pairs={{0,4},{2,6},{4,8},{6,10},{8,12},{10,14},{12,16},{14,18},{16,20},{1... | collective-permute-start | bytes 1572872 | tf_op jit(solution)/shard_map/ppermute | solution.py:22
  59.3 24.4 %collective-permute-start.7 = (bf16[2,128,1024]{1,2,0:T(8,128)(2,1)S(1)}, bf16[2,128,1024]{1,2,0:T(8,128)(2,1)S(1)}, u32[]{:S(2)}, u32[]{:S(2)}) collective-permute-start(bf16[2,128,1024]{1,2,0:T(8,128)(2,1)S(1)} %pad_maximum_fusion.1), channel_id=1, source_target_pairs={{0,2},{2,4},{4,6},{6,8},{8,10},{10,12},{12,14},{14,16},{16,18},{18... | collective-permute-start | bytes 1572872 | tf_op jit(solution)/shard_map/ppermute | solution.py:22
  84.0 1.8 copy-start.5
  100.3 12.1 %copy-start.7 = (f32[5376]{0:T(1024)S(1)}, f32[5376]{0:T(1024)}, u32[]{:S(2)}) copy-start(f32[5376]{0:T(1024)} %param.39) | copy-start | bytes 64516
  110.7 98.2 %copy-start.3 = (bf16[128,2688]{1,0:T(8,128)(2,1)S(1)}, bf16[128,2688]{1,0:T(8,128)(2,1)}, u32[]{:S(2)}) copy-start(bf16[128,2688]{1,0:T(8,128)(2,1)} %param.34) | copy-start | bytes 2064388
  112.3 152.8 %all-gather.6.cloned.1.call-start = ((), (), s32[]{:S(2)}) async-start(), calls=%async_computation.1 | async-start | bytes 2064384 | tf_op jit(solution)/shard_map/all_gather | solution.py:242
  208.9 197.8 %copy-start.6 = (f32[5376]{0:T(1024)S(1)}, f32[5376]{0:T(1024)}, u32[]{:S(2)}) copy-start(f32[5376]{0:T(1024)} %param.40) | copy-start | bytes 64516
  209.2 203.7 %copy-start.2 = (bf16[128,2688]{1,0:T(8,128)(2,1)}, bf16[128,2688]{1,0:T(8,128)(2,1)S(1)}, u32[]{:S(2)}) copy-start(bf16[128,2688]{1,0:T(8,128)(2,1)S(1)} %fusion.119) | copy-start | bytes 2064388
  209.3 10.3 collective-permute-start.8
  219.6 9.4 collective-permute-start.9
  229.0 8.5 collective-permute-start.10
  237.6 15.9 %collective-permute-start.11 = (bf16[64,2688]{1,0:T(8,128)(2,1)S(1)}, bf16[64,2688]{1,0:T(8,128)(2,1)S(1)}, u32[]{:S(2)}, u32[]{:S(2)}) collective-permute-start(bf16[64,2688]{1,0:T(8,128)(2,1)S(1)} %collective-permute-done.10), channel_id=1, source_target_pairs={{0,16},{16,0},{2,18},{18,2},{4,20},{20,4},{6,22},{22,6},{8,24},{24... | collective-permute-start | bytes 1032200 | tf_op jit(solution)/shard_map/ppermute | solution.py:32
  254.3 152.4 %all-gather.8.cloned.1.call-start = ((), (), s32[]{:S(2)}) async-start(), calls=%async_computation.2 | async-start | bytes 11698176 | tf_op jit(solution)/shard_map/all_gather | solution.py:138
  255.1 290.1 %all-gather.10.cloned.1.call-start = ((), (), s32[]{:S(2)}) async-start(), calls=%async_computation.3 | async-start | bytes 11698176 | tf_op jit(solution)/shard_map/all_gather | solution.py:149
  255.7 532.1 %all-gather.14.cloned.1.call-start = ((), (), s32[]{:S(2)}) async-start(), calls=%async_computation.5 | async-start | bytes 23396352 | tf_op jit(solution)/shard_map/all_gather | solution.py:125
  256.2 646.1 %all-gather.12.cloned.1.call-start = ((), (), s32[]{:S(2)}) async-start(), calls=%async_computation.4 | async-start | bytes 8912896 | tf_op jit(solution)/shard_map/all_gather | solution.py:261
  266.8 278.3 %copy-start.1 = (bf16[128,5376]{1,0:T(8,128)(2,1)S(1)}, bf16[128,5376]{1,0:T(8,128)(2,1)}, u32[]{:S(2)}) copy-start(bf16[128,5376]{1,0:T(8,128)(2,1)} %all-gather.6.cloned.1.call-done) | copy-start | bytes 4128772
Sparse Core Ops, SparseCore 0:
  112.4 92.2 reduce-scatter.3
  254.5 10.6 all-gather.5
  268.3 138.3 all-gather.7
  409.7 135.3 all-gather.9
  548.2 239.5 all-gather.13
  791.3 110.9 all-gather.11
where the time goes:
time: 1090 us
  waiting for transfers between devices  758 us (70%)
  loops' own time  83.9 us (8%)
  matrix products  74.2 us (7%)
  local copies, waits for them, and re-layouts  71.1 us (7%)
  starting transfers between devices  58 us (5%)
  other arithmetic  29.5 us (3%)
  between operations  14.7 us (1%)
    all_gather x1, waiting for transfers between devices, project(): lax.all_gather(proj_query, 'ctx', axis=0, tiled=True)  236 us
    all_gather x1, waiting for transfers between devices, project(): lax.all_gather(key_projection, 'ctx', axis=0, tiled=True)  140 us
    all_gather x1, waiting for transfers between devices, project(): lax.all_gather(value_projection, 'ctx', axis=0, tiled=True)  132 us
    all_gather x1, waiting for transfers between devices, shards(): piece = lax.all_gather(pair_two, 'ctx', axis=1, tiled=True)  104 us
    unnamed x7, waiting for transfers between devices  94.1 us
    another operation x1, loops' own time, shards(): final_state = lax.fori_loop(0, unit_count, one_unit, start_state)  81.6 us
    ppermute x8, starting transfers between devices, shifted(): lax.ppermute(value, axis, [(source, source + steps) for source in range(l...  49.6 us
    ppermute x4, waiting for transfers between devices, from_partner(): return lax.ppermute(block, axis, route)  36.2 us
  transfers between devices with their start and end apart: 18, of which 11 were waited for; matrix products, arithmetic and copies ran while one was open for 4% of the time, Pallas kernels for 0%

commit v1 on v0

--- a/solution.py
+++ b/solution.py
@@ -3,6 +3,8 @@
 import jax
 import jax.numpy as jnp
 from jax import lax
+from jax.experimental import pallas as pl
+from jax.experimental.pallas import tpu as pltpu
 from jax.sharding import PartitionSpec as P
 
 MODEL_WIDTH = 5376
@@ -304,6 +306,494 @@
     return (resid_out, attended)
 
 
+MESH = pl.DeviceIdType.MESH
+QUERY_TILE = 256
+
+
+def spread_fits(mesh):
+    return mesh.shape["heads"] == 2 and mesh.shape["ctx"] == 16
+
+
+def greet_all(count):
+    me, core = lax.axis_index("ctx"), lax.axis_index("heads")
+    barrier = pltpu.get_barrier_semaphore()
+
+    def greet(step, carry):
+        pl.semaphore_signal(
+            barrier, inc=1, device_id=(lax.rem(me + step, count), core), device_id_type=MESH
+        )
+        pl.semaphore_signal(
+            barrier, inc=1, device_id=(lax.rem(me + step, count), 1 - core), device_id_type=MESH
+        )
+        return carry
+
+    lax.fori_loop(1, count, greet, 0)
+    pl.semaphore_signal(barrier, inc=1, device_id=(me, 1 - core), device_id_type=MESH)
+    pl.semaphore_wait(barrier, 2 * count - 1)
+
+
+def attend_tile(tile, band, query_ref, key_ref, value_ref, low_ref, mixed_ref):
+    tokens = query_ref.shape[0]
+    span = min(band + QUERY_TILE, tokens)
+    first = pl.multiple_of(tile * QUERY_TILE, QUERY_TILE)
+    begin = pl.multiple_of(jnp.maximum(first + QUERY_TILE - span, 0), QUERY_TILE)
+    scores = (
+        lax.dot_general(
+            query_ref[pl.ds(first, QUERY_TILE), :],
+            key_ref[pl.ds(begin, span), :],
+            (((1,), (1,)), ((), ())),
+            preferred_element_type=jnp.float32,
+        )
+        * SCALE
+    )
+    rows = first + lax.broadcasted_iota(jnp.int32, (QUERY_TILE, 1), 0)
+    columns = begin + lax.broadcasted_iota(jnp.int32, (1, span), 1)
+    visible = (columns <= rows) & (columns >= low_ref[pl.ds(first, QUERY_TILE), :])
+    scores = jnp.where(visible, scores, -1e30)
+    lifted = jnp.exp(scores - jnp.max(scores, axis=1, keepdims=True))
+    total = jnp.sum(lifted, axis=1, keepdims=True)
+    mixed = jnp.dot(
+        lifted.astype(jnp.bfloat16),
+        value_ref[pl.ds(begin, span), :],
+        preferred_element_type=jnp.float32,
+    )
+    mixed_ref[pl.ds(first, QUERY_TILE), :] = (mixed / total).astype(jnp.bfloat16)
+
+
+def first_kernel(
+    count,
+    band,
+    query_in,
+    key_in,
+    value_in,
+    low_ref,
+    wq_ref,
+    wk_ref,
+    wv_ref,
+    attend_out,
+    weight_out,
+    query_all,
+    key_all,
+    value_all,
+    mixed,
+    in_send,
+    in_recv,
+    in_own,
+    back_send,
+    back_recv,
+    back_own,
+    w_send,
+    w_recv,
+    w_own,
+):
+    me, core = lax.axis_index("ctx"), lax.axis_index("heads")
+    tok = query_in.shape[0]
+    depth = wq_ref.shape[0]
+    half = count // 2
+    greet_all(count)
+
+    def columns(index):
+        return pl.ds(pl.multiple_of(index * HEAD_SIZE, HEAD_SIZE), HEAD_SIZE)
+
+    def rows(index, size=tok):
+        return pl.ds(pl.multiple_of(index * size, size), size)
+
+    def inward(step):
+        to = lax.rem(me + step, count)
+        trio = (
+            (query_in, query_all, to),
+            (key_in, key_all, to // 2),
+            (value_in, value_all, to // 2),
+        )
+        return [
+            pltpu.make_async_remote_copy(
+                src_ref=source.at[:, columns(block)],
+                dst_ref=target.at[rows(me), :],
+                send_sem=in_send.at[kind, step],
+                recv_sem=in_recv.at[kind, step],
+                device_id=(to, core),
+                device_id_type=MESH,
+            )
+            for kind, (source, target, block) in enumerate(trio)
+        ]
+
+    def start_inward(step, carry):
+        for copy in inward(step):
+            copy.start()
+        return carry
+
+    def wait_inward(step, carry):
+        for copy in inward(step):
+            copy.wait()
+        return carry
+
+    lax.fori_loop(1, count, start_inward, 0)
+    own = [
+        pltpu.make_async_copy(source.at[:, columns(block)], target.at[rows(me), :], in_own.at[kind])
+        for kind, (source, target, block) in enumerate(
+            (
+                (query_in, query_all, me),
+                (key_in, key_all, me // 2),
+                (value_in, value_all, me // 2),
+            )
+        )
+    ]
+    for copy in own:
+        copy.start()
+    for copy in own:
+        copy.wait()
+    lax.fori_loop(1, count, wait_inward, 0)
+
+    to_core = me // half
+    place = lax.rem(me, half)
+    apart = jnp.where(to_core == core, 0, 1)
+
+    def weight_views(pair, odd):
+        to = 2 * pair + odd
+        base = pl.multiple_of(apart * 2 * HEAD_SIZE, HEAD_SIZE)
+        next_base = pl.multiple_of(apart * 2 * HEAD_SIZE + HEAD_SIZE, HEAD_SIZE)
+        second = wk_ref if odd == 0 else wv_ref
+        return (
+            (wq_ref.at[:, columns(to)], weight_out.at[rows(place, depth), pl.ds(base, HEAD_SIZE)]),
+            (
+                second.at[:, columns(pair)],
+                weight_out.at[rows(place, depth), pl.ds(next_base, HEAD_SIZE)],
+            ),
+        )
+
+    def weight_remote(pair, odd):
+        to = 2 * pair + odd
+        return [
+            pltpu.make_async_remote_copy(
+                src_ref=source,
+                dst_ref=target,
+                send_sem=w_send.at[kind, to],
+                recv_sem=w_recv.at[kind, place * 2 + apart],
+                device_id=(to, to_core),
+                device_id_type=MESH,
+            )
+            for kind, (source, target) in enumerate(weight_views(pair, odd))
+        ]
+
+    def weight_local(pair, odd):
+        return [
+            pltpu.make_async_copy(source, target, w_own.at[kind])
+            for kind, (source, target) in enumerate(weight_views(pair, odd))
+        ]
+
+    def each_weight(act_remote, act_local):
+        def body(pair, carry):
+            for odd in range(2):
+                to = 2 * pair + odd
+                mine = (to == me) & (to_core == core)
+
+                @pl.when(jnp.logical_not(mine))
+                def _():
+                    for copy in weight_remote(pair, odd):
+                        act_remote(copy)
+
+                @pl.when(mine)
+                def _():
+                    for copy in weight_local(pair, odd):
+                        act_local(copy)
+
+            return carry
+
+        lax.fori_loop(0, half, body, 0)
+
+    each_weight(lambda copy: copy.start(), lambda copy: copy.start())
+
+    def outward(to):
+        return pltpu.make_async_remote_copy(
+            src_ref=mixed.at[rows(to), :],
+            dst_ref=attend_out.at[:, columns(me)],
+            send_sem=back_send.at[to],
+            recv_sem=back_recv.at[me],
+            device_id=(to, core),
+            device_id_type=MESH,
+        )
+
+    def outward_own():
+        return pltpu.make_async_copy(
+            mixed.at[rows(me), :], attend_out.at[:, columns(me)], back_own
+        )
+
+    per_tile = QUERY_TILE // tok
+
+    def one_tile(tile, carry):
+        attend_tile(tile, band, query_all, key_all, value_all, low_ref, mixed)
+        for part in range(per_tile):
+            to = tile * per_tile + part
+
+            @pl.when(to != me)
+            def _():
+                outward(to).start()
+
+            @pl.when(to == me)
+            def _():
+                outward_own().start()
+
+        return carry
+
+    lax.fori_loop(0, count // per_tile, one_tile, 0)
+
+    def finish(step, carry):
+        to = lax.rem(me + step, count)
+        outward(to).wait_send()
+        pltpu.make_async_remote_copy(
+            src_ref=mixed.at[rows(to), :],
+            dst_ref=attend_out.at[:, columns(to)],
+            send_sem=back_send.at[to],
+            recv_sem=back_recv.at[to],
+            device_id=(to, core),
+            device_id_type=MESH,
+        ).wait_recv()
+        return carry
+
+    lax.fori_loop(1, count, finish, 0)
+    outward_own().wait()
+    each_weight(lambda copy: copy.wait_send(), lambda copy: copy.wait())
+
+    def weight_arrived(slot, carry):
+        from_place, from_apart = slot // 2, lax.rem(slot, 2)
+        sender = core * half + from_place
+        mine = (sender == me) & (from_apart == 0)
+
+        @pl.when(jnp.logical_not(mine))
+        def _():
+            for kind in range(2):
+                left = pl.multiple_of((from_apart * 2 + kind) * HEAD_SIZE, HEAD_SIZE)
+                view = weight_out.at[rows(from_place, depth), pl.ds(left, HEAD_SIZE)]
+                pltpu.make_async_remote_copy(
+                    src_ref=view,
+                    dst_ref=view,
+                    send_sem=w_send.at[kind, 0],
+                    recv_sem=w_recv.at[kind, slot],
+                    device_id=(me, 1 - core),
+                    device_id_type=MESH,
+                ).wait_recv()
+
+        return carry
+
+    lax.fori_loop(0, count, weight_arrived, 0)
+
+
+def first_attention(count, band, queries, keys, values, low, wq, wk, wv):
+    tok = queries.shape[0]
+    tokens = tok * count
+    whole = (tokens, HEAD_SIZE)
+    dma = pltpu.SemaphoreType.DMA
+    vmem = pl.BlockSpec(memory_space=pltpu.VMEM)
+    anywhere = pl.BlockSpec(memory_space=pl.ANY)
+    return pl.pallas_call(
+        partial(first_kernel, count, band),
+        out_shape=(
+            jax.ShapeDtypeStruct(queries.shape, jnp.bfloat16),
+            jax.ShapeDtypeStruct((wq.shape[0] * count // 2, 4 * HEAD_SIZE), jnp.bfloat16),
+        ),
+        in_specs=[vmem] * 4 + [anywhere] * 3,
+        out_specs=(anywhere, anywhere),
+        scratch_shapes=[pltpu.VMEM(whole, jnp.bfloat16)] * 4
+        + [
+            dma((3, count)),
+            dma((3, count)),
+            dma((3,)),
+            dma((count,)),
+            dma((count,)),
+            dma,
+            dma((2, count)),
+            dma((2, count)),
+            dma((2,)),
+        ],
+        compiler_params=pltpu.CompilerParams(
+            collective_id=0, has_side_effects=True, vmem_limit_bytes=48 * 1024 * 1024
+        ),
+        name="first_attention",
+    )(queries, keys, values, low, wq, wk, wv)
+
+
+def second_kernel(
+    count, band, query_ref, key_ref, value_ref, low_ref, attend_out, mixed, back_send, back_recv, back_own
+):
+    me, core = lax.axis_index("ctx"), lax.axis_index("heads")
+    half = attend_out.shape[0] // 2
+    blocks = 2 * count
+    greet_all(count)
+    own_columns = pl.ds(pl.multiple_of(me * HEAD_SIZE, HEAD_SIZE), HEAD_SIZE)
+
+    def home(block):
+        odd = lax.rem(block, 2)
+        return jnp.where(odd == 0, block // 2, (blocks - 1 - block) // 2), odd
+
+    def rows(index):
+        return pl.ds(pl.multiple_of(index * half, half), half)
+
+    def outward(block, to, odd):
+        return pltpu.make_async_remote_copy(
+            src_ref=mixed.at[rows(block), :],
+            dst_ref=attend_out.at[rows(odd), own_columns],
+            send_sem=back_send.at[block],
+            recv_sem=back_recv.at[odd, me],
+            device_id=(to, core),
+            device_id_type=MESH,
+        )
+
+    def outward_own(block, odd):
+        return pltpu.make_async_copy(
+            mixed.at[rows(block), :], attend_out.at[rows(odd), own_columns], back_own.at[odd]
+        )
+
+    per_tile = QUERY_TILE // half
+
+    def one_tile(tile, carry):
+        attend_tile(tile, band, query_ref, key_ref, value_ref, low_ref, mixed)
+        for part in range(per_tile):
+            block = tile * per_tile + part
+            to, odd = home(block)
+
+            @pl.when(to != me)
+            def _():
+                outward(block, to, odd).start()
+
+            @pl.when(to == me)
+            def _():
+                outward_own(block, odd).start()
+
+        return carry
+
+    lax.fori_loop(0, blocks // per_tile, one_tile, 0)
+
+    def finish(block, carry):
+        to, odd = home(block)
+
+        @pl.when(to != me)
+        def _():
+            outward(block, to, odd).wait_send()
+
+        @pl.when(to == me)
+        def _():
+            outward_own(block, odd).wait()
+
+        return carry
+
+    lax.fori_loop(0, blocks, finish, 0)
+
+    def arrived(step, carry):
+        sender = lax.rem(me + step, count)
+        left = pl.multiple_of(sender * HEAD_SIZE, HEAD_SIZE)
+        for odd in range(2):
+            view = attend_out.at[pl.ds(odd * half, half), pl.ds(left, HEAD_SIZE)]
+            pltpu.make_async_remote_copy(
+                src_ref=view,
+                dst_ref=view,
+                send_sem=back_send.at[0],
+                recv_sem=back_recv.at[odd, sender],
+                device_id=(sender, core),
+                device_id_type=MESH,
+            ).wait_recv()
+        return carry
+
+    lax.fori_loop(1, count, arrived, 0)
+
+
+def second_attention(count, band, queries, keys, values, low):
+    tokens = queries.shape[0]
+    dma = pltpu.SemaphoreType.DMA
+    vmem = pl.BlockSpec(memory_space=pltpu.VMEM)
+    return pl.pallas_call(
+        partial(second_kernel, count, band),
+        out_shape=jax.ShapeDtypeStruct((tokens // count, count * HEAD_SIZE), jnp.bfloat16),
+        in_specs=[vmem] * 4,
+        out_specs=pl.BlockSpec(memory_space=pl.ANY),
+        scratch_shapes=[
+            pltpu.VMEM((tokens, HEAD_SIZE), jnp.bfloat16),
+            dma((2 * count,)),
+            dma((2, count)),
+            dma((2,)),
+        ],
+        compiler_params=pltpu.CompilerParams(
+            collective_id=1, has_side_effects=True, vmem_limit_bytes=48 * 1024 * 1024
+        ),
+        name="second_attention",
+    )(queries, keys, values, low)
+
+
+def to_other_core(block):
+    return lax.ppermute(block, "heads", [(0, 1), (1, 0)])
+
+
+def shards_by_head(
+    count,
+    resid_in,
+    first_layer_queries,
+    first_layer_keys,
+    first_layer_values,
+    out_one,
+    post_gain,
+    pre_gain,
+    proj_query,
+    key_projection,
+    value_projection,
+    window,
+    positions,
+):
+    me, core = lax.axis_index("ctx"), lax.axis_index("heads")
+    col_width = resid_in.shape[1]
+    tokens = positions.shape[0]
+    token = jnp.arange(tokens, dtype=jnp.int32)
+    document = token - positions
+    own_window = lax.dynamic_index_in_dim(window, me, 0, keepdims=False)
+    low_one = jnp.maximum(document, token - own_window + 1)
+    resid_other = to_other_core(resid_in)
+    attend_one, weights = first_attention(
+        count,
+        LONGEST_WINDOW,
+        first_layer_queries,
+        first_layer_keys,
+        first_layer_values,
+        low_one[:, None],
+        proj_query,
+        key_projection,
+        value_projection,
+    )
+    partial_rows = jnp.dot(attend_one, out_one, preferred_element_type=jnp.float32).astype(
+        jnp.bfloat16
+    )
+    combined = partial_rows.astype(jnp.float32) + to_other_core(partial_rows).astype(jnp.float32)
+    post_scaled = combined * lax.rsqrt(
+        jnp.mean(combined * combined, axis=1, keepdims=True) + EPS
+    )
+    resid_row = jnp.where(
+        core == 0,
+        jnp.concatenate([resid_in, resid_other], axis=1),
+        jnp.concatenate([resid_other, resid_in], axis=1),
+    )
+    resid_full = (resid_row.astype(jnp.float32) + post_gain[None, :] * post_scaled).astype(
+        jnp.bfloat16
+    )
+    resid_out = lax.dynamic_slice_in_dim(resid_full, core * col_width, col_width, 1)
+    widened = resid_full.astype(jnp.float32)
+    factor = lax.rsqrt(jnp.mean(widened * widened, axis=1, keepdims=True) + EPS)
+    gain_slice = lax.dynamic_slice_in_dim(pre_gain, core * col_width, col_width, 0)
+    normed = (gain_slice[None, :] * resid_out.astype(jnp.float32) * factor).astype(jnp.bfloat16)
+    gathered = lax.all_gather(normed, "ctx", axis=0, tiled=True)
+    away = jnp.dot(gathered, weights[:, 2 * HEAD_SIZE :], preferred_element_type=jnp.float32)
+    arrived = to_other_core(away)
+    kept = jnp.dot(gathered, weights[:, : 2 * HEAD_SIZE], preferred_element_type=jnp.float32)
+    product = (kept + arrived).reshape(tokens, 2, HEAD_SIZE)
+    rotated = apply_rotary(product, positions, POSITION_FACTOR).astype(jnp.bfloat16)
+    even = lax.rem(me, 2) == 0
+    query_two = rotated[:, 0]
+    mine = jnp.where(even, rotated[:, 1], product[:, 1].astype(jnp.bfloat16))
+    theirs = from_partner(mine, "ctx", 0)
+    key_two = jnp.where(even, mine, theirs)
+    value_two = jnp.where(even, theirs, mine)
+    attended = second_attention(
+        count, tokens // 2, query_two, key_two, value_two, document[:, None]
+    )
+    return (resid_out, attended)
+
+
 def solution(mesh):
     placed = (
         P("ctx", "heads"),
@@ -320,7 +810,9 @@
         P(),
     )
     return jax.shard_map(
-        shards,
+        partial(shards_by_head, mesh.shape["ctx"])
+        if spread_fits(mesh)
+        else shards,
         mesh=mesh,
         in_specs=placed,
         out_specs=(P("ctx", "heads"), P("ctx", "heads")),

time: 1090 us -> 378 us (0.35)
  waiting for transfers between devices: 758 us -> 169 us
  Pallas kernels: 0 us -> 135 us
  loops' own time: 83.9 us -> 0 us
  starting transfers between devices: 58 us -> 2.12 us
  local copies, waits for them, and re-layouts: 71.1 us -> 16.5 us
  matrix products: 74.2 us -> 27 us
  other arithmetic: 29.5 us -> 14.9 us
    all_gather x5 -> x1, waiting for transfers between devices: 619 us -> 153 us  [shards_by_head(): gathered = lax.all_gather(normed, 'ctx', axis=0, tiled=True)]
    pallas_call x0 -> x2, Pallas kernels: none -> 135 us  [the longest x1 115 us: first_attention(): pl.pallas_call(partial(first_kernel, count, band), out_shape=(jax.ShapeDt...]
    unnamed x7 -> x1, waiting for transfers between devices: 94.1 us -> 0.02 us
    another operation x65 -> x0, loops' own time: 83.9 us -> none  [the longest x1 81.6 us: shards(): final_state = lax.fori_loop(0, unit_count, one_unit, start_state)]
    ppermute x8 -> x3, starting transfers between devices: 49.6 us -> 0.56 us  [to_other_core(): return lax.ppermute(block, 'heads', [(0, 1), (1, 0)])]
    dot_general x71 -> x3, matrix products: 63.2 us -> 27 us  [the longest x1 10.4 us: shards_by_head(): jnp.dot(attend_one, out_one, preferred_element_type=jnp.float32)]
    gather x35 -> x0, local copies, waits for them, and re-layouts: 34 us -> none  [lookup(): jnp.take(position_table, jnp.clip(tokens, 0, position_table.shape[0] - 1))]
    ppermute x4 -> x1, waiting for transfers between devices: 36.2 us -> 12.5 us  [from_partner(): return lax.ppermute(block, axis, route)]
  transfers between devices with their start and end apart: 18 -> 5, of which waited for: 11 -> 3; matrix products, arithmetic and copies ran while one was open for 4% -> 2% of each run, Pallas kernels for 0% -> 0%
where the time goes in v1:
time: 378 us
  waiting for transfers between devices  169 us (45%)
  Pallas kernels  135 us (36%)
  matrix products  27 us (7%)
  local copies, waits for them, and re-layouts  16.5 us (4%)
  other arithmetic  14.9 us (4%)
  between operations  14.2 us (4%)
    all_gather x1, waiting for transfers between devices, shards_by_head(): gathered = lax.all_gather(normed, 'ctx', axis=0, tiled=True)  153 us
    pallas_call x1, Pallas kernels, first_attention(): pl.pallas_call(partial(first_kernel, count, band), out_shape=(jax.ShapeDt...  115 us
    pallas_call x1, Pallas kernels, second_attention(): pl.pallas_call(partial(second_kernel, count, band), out_shape=jax.ShapeDt...  19.1 us
    ppermute x1, waiting for transfers between devices, from_partner(): return lax.ppermute(block, axis, route)  12.5 us
    unnamed x26, local copies, waits for them, and re-layouts  12.4 us
    dot_general x1, matrix products, shards_by_head(): jnp.dot(attend_one, out_one, preferred_element_type=jnp.float32)  10.4 us
    dot_general x1, matrix products, shards_by_head(): jnp.dot(gathered, weights[:, 2 * HEAD_SIZE:], preferred_element_type=jnp....  8.67 us
    dot_general x1, matrix products, shards_by_head(): jnp.dot(gathered, weights[:, :2 * HEAD_SIZE], preferred_element_type=jnp....  7.94 us
  transfers between devices with their start and end apart: 5, of which 3 were waited for; matrix products, arithmetic and copies ran while one was open for 2% of the time, Pallas kernels for 0%

profile of v1, /device:TPU:0, one launch (start us, length us, event | category | flops | bytes accessed | tf_op | source)
XLA Modules:
  0.0 377.9 jit_solution(13554072371840849460)
XLA Ops:
  7.2 1.2 dynamic_slice.10
  8.5 1.3 iota_subtract_fusion
  9.8 0.4 copy.15.low_ref
  10.2 1.3 copy-done
  11.5 1.1 copy-done.1
  12.6 1.1 copy-done.2
  13.7 1.0 copy-done.3
  14.8 0.9 copy-done.4
  15.7 0.9 copy-done.5
  16.7 115.5 %first_attention.1 = (bf16[128,2048]{1,0:T(8,128)(2,1)S(1)}, bf16[2688,512]{1,0:T(8,128)(2,1)}) custom-call(bf16[128,2048]{1,0:T(8,128)(2,1)S(1)} %copy-done.3, bf16[128,1024]{1,0:T(8,128)(2,1)S(1)} %copy-done.4, bf16[128,1024]{1,0:T(8,128)(2,1)S(1)} %copy-done.5, s32[2048,1]{1,0:T(8,128)S(1)} %copy.15.low_ref, bf16[336,2048]{1,0:T(8,128)(2,1)S(1)} %copy-done, ...), custom_call_target="tpu_custom_call" | custom-call | tf_op jit(solution)/shard_map/first_attention/pallas_call | solution.py:588
  132.2 10.4 %convolution_convert_fusion = bf16[128,5376]{1,0:T(8,128)(2,1)S(1)} fusion(bf16[128,2048]{1,0:T(8,128)(2,1)S(1)} %get-tuple-element.4, bf16[2048,5376]{1,0:T(8,128)(2,1)} %param.16), kind=kOutput, calls=%fused_computation | convolution fusion | flops 2819260416 | bytes 23920640 | tf_op jit(solution)/shard_map/dot_general | solution.py:759
  142.6 0.5 collective-permute-start
  143.2 3.5 collective-permute-done.1
  146.7 0.5 multiply_reduce_fusion.1
  147.3 2.7 multiply_reduce_fusion
  150.0 1.3 multiply_convert_fusion
  151.3 152.6 %all-gather.2.cloned.1.call-done = bf16[2048,2688]{1,0:T(8,128)(2,1)} async-done(((bf16[128,2688]{1,0:T(8,128)(2,1)}), bf16[2048,2688]{1,0:T(8,128)(2,1)}) %all-gather.2.cloned.1.call-update) | async-done | bytes 11010064 | tf_op jit(solution)/shard_map/all_gather | solution.py:779
  304.0 8.7 %fusion = f32[2048,256]{0,1:T(8,128)} fusion(bf16[2048,2688]{1,0:T(8,128)(2,1)} %all-gather.2.cloned.1.call-done, bf16[2688,512]{1,0:T(8,128)(2,1)S(1)} %copy-done.10), kind=kOutput, calls=%fused_computation.11 | convolution fusion | flops 2818572288 | bytes 14483456 | tf_op jit(solution)/shard_map/dot_general | solution.py:780
  312.7 5.5 %multiply_cosine_fusion = (f32[2048,64]{1,0:T(8,128)}, f32[2048,64]{1,0:T(8,128)}) fusion(f32[64]{0:T(128)S(1)} %negate_power_fusion, f32[2048]{0:T(1024)S(1)} %convert_multiply_fusion), kind=kLoop, calls=%fused_computation.9 | loop fusion | flops 131072 | bytes 1057024 | tf_op jit(solution)/shard_map/cos | solution.py:41
  318.2 7.9 %convolution_add_fusion = f32[2048,256]{0,1:T(8,128)S(1)} fusion(f32[2048,256]{0,1:T(8,128)} %collective-permute-done.2, bf16[2048,2688]{1,0:T(8,128)(2,1)} %all-gather.2.cloned.1.call-done, bf16[2688,512]{1,0:T(8,128)(2,1)S(1)} %copy-done.10), kind=kOutput, calls=%fused_computation.5 | convolution fusion | flops 2819096576 | bytes 16580608 | tf_op jit(solution)/shard_map/dot_general | solution.py:782
  326.2 1.2 fusion.7
  327.4 0.9 slice.33
  328.2 1.8 copy.22
  330.1 1.9 copy.23
  332.0 1.3 copy.24
  333.3 2.7 add_convert_fusion.1
  336.0 0.6 fusion.6
  336.7 1.5 collective-permute-start.3
  338.2 0.4 copy.20.low_ref
  338.6 12.5 %collective-permute-done.3 = bf16[2048,128]{1,0:T(8,128)(2,1)S(1)} collective-permute-done((bf16[2048,128]{1,0:T(8,128)(2,1)S(1)}, bf16[2048,128]{1,0:T(8,128)(2,1)S(1)}, u32[]{:S(2)}, u32[]{:S(2)}) %collective-permute-start.3) | collective-permute-done | bytes 524320 | tf_op jit(solution)/shard_map/ppermute | solution.py:34
  351.2 19.1 %second_attention.1 = bf16[128,2048]{1,0:T(8,128)(2,1)S(1)} custom-call(bf16[2048,128]{1,0:T(8,128)(2,1)S(1)} %get-tuple-element.13.query_ref, bf16[2048,128]{1,0:T(8,128)(2,1)S(1)} %get-tuple-element.17.key_ref, bf16[2048,128]{1,0:T(8,128)(2,1)S(1)} %get-tuple-element.16.value_ref, s32[2048,1]{1,0:T(8,128)S(1)} %copy.20.low_ref), custom_call_target="tpu_custom_call" | custom-call | tf_op jit(solution)/shard_map/second_attention/pallas_call | solution.py:703
  370.3 0.8 copy.26
  (28 shorter events, 0.3 us)
Async XLA Ops:
  7.2 296.8 %all-gather.2.cloned.1.call-start = ((), (), s32[]{:S(2)}) async-start(), calls=%async_computation | async-start | bytes 11698176 | tf_op jit(solution)/shard_map/all_gather | solution.py:779
  10.2 1.3 copy-start
  11.5 1.1 copy-start.1
  12.6 1.1 copy-start.2
  13.7 1.0 copy-start.3
  14.8 0.9 copy-start.4
  15.7 0.9 copy-start.5
  132.1 10.5 %copy-start.6 = (bf16[128,2688]{1,0:T(8,128)(2,1)S(1)}, bf16[128,2688]{1,0:T(8,128)(2,1)}, u32[]{:S(2)}) copy-start(bf16[128,2688]{1,0:T(8,128)(2,1)} %param.12) | copy-start | bytes 2064388
  132.1 11.0 %copy-start.9 = (f32[5376]{0:T(1024)S(1)}, f32[5376]{0:T(1024)}, u32[]{:S(2)}) copy-start(f32[5376]{0:T(1024)} %param.18) | copy-start | bytes 64516
  142.5 4.8 %copy-start.8 = (f32[5376]{0:T(1024)S(1)}, f32[5376]{0:T(1024)}, u32[]{:S(2)}) copy-start(f32[5376]{0:T(1024)} %param.17) | copy-start | bytes 64516
  142.5 4.2 %collective-permute-start.1 = (bf16[128,5376]{1,0:T(8,128)(2,1)S(1)}, bf16[128,5376]{1,0:T(8,128)(2,1)S(1)}, u32[]{:S(2)}, u32[]{:S(2)}) collective-permute-start(bf16[128,5376]{1,0:T(8,128)(2,1)S(1)} %convolution_convert_fusion), channel_id=1, source_target_pairs={{0,1},{1,0},{2,3},{3,2},{4,5},{5,4},{6,7},{7,6},{8,9},{9,8},{10,11... | collective-permute-start | bytes 4128776 | tf_op jit(solution)/shard_map/ppermute | solution.py:722
  142.6 4.6 %collective-permute-start = (bf16[128,2688]{1,0:T(8,128)(2,1)S(1)}, bf16[128,2688]{1,0:T(8,128)(2,1)}, u32[]{:S(2)}, u32[]{:S(2)}) collective-permute-start(bf16[128,2688]{1,0:T(8,128)(2,1)S(1)} %copy-done.6), channel_id=1, source_target_pairs={{0,1},{1,0},{2,3},{3,2},{4,5},{5,4},{6,7},{7,6},{8,9},{9,8},{10,11... | collective-permute-start | bytes 2064392 | tf_op jit(solution)/shard_map/ppermute | solution.py:722
  150.0 154.0 %copy-start.10 = (bf16[2688,512]{1,0:T(8,128)(2,1)S(1)}, bf16[2688,512]{1,0:T(8,128)(2,1)}, u32[]{:S(2)}) copy-start(bf16[2688,512]{1,0:T(8,128)(2,1)} %get-tuple-element.5) | copy-start | bytes 8257540
  304.0 8.7 %copy-start.7 = (s32[2048]{0:T(1024)S(1)}, s32[2048]{0:T(1024)}, u32[]{:S(2)}) copy-start(s32[2048]{0:T(1024)} %param.23) | copy-start | bytes 24580
  312.7 5.6 %collective-permute-start.2 = (f32[2048,256]{0,1:T(8,128)}, f32[2048,256]{0,1:T(8,128)}, u32[]{:S(2)}, u32[]{:S(2)}) collective-permute-start(f32[2048,256]{0,1:T(8,128)} %fusion), channel_id=1, source_target_pairs={{0,1},{1,0},{2,3},{3,2},{4,5},{5,4},{6,7},{7,6},{8,9},{9,8},{10,11... | collective-permute-start | bytes 6291464 | tf_op jit(solution)/shard_map/ppermute | solution.py:722
  336.7 14.4 %collective-permute-start.3 = (bf16[2048,128]{1,0:T(8,128)(2,1)S(1)}, bf16[2048,128]{1,0:T(8,128)(2,1)S(1)}, u32[]{:S(2)}, u32[]{:S(2)}) collective-permute-start(bf16[2048,128]{1,0:T(8,128)(2,1)S(1)} %get-tuple-element.12), channel_id=1, source_target_pairs={{0,2},{2,0},{4,6},{6,4},{8,10},{10,8},{12,14},{14,12},{16,18},{18,... | collective-permute-start | bytes 1572872 | tf_op jit(solution)/shard_map/ppermute | solution.py:34
Sparse Core Ops, SparseCore 0:
  151.5 152.4 all-gather.1

commit v2 on v1

--- a/solution.py
+++ b/solution.py
@@ -613,12 +613,220 @@
 
 
 def second_kernel(
-    count, band, query_ref, key_ref, value_ref, low_ref, attend_out, mixed, back_send, back_recv, back_own
+    count,
+    band,
+    normed_ref,
+    weight_ref,
+    cosine_ref,
+    sine_ref,
+    low_ref,
+    attend_out,
+    held,
+    kept,
+    away,
+    arrived,
+    query_all,
+    pair_all,
+    mixed,
+    hop_send,
+    hop_recv,
+    core_send,
+    core_recv,
+    pair_send,
+    pair_recv,
+    back_send,
+    back_recv,
+    back_own,
 ):
     me, core = lax.axis_index("ctx"), lax.axis_index("heads")
-    half = attend_out.shape[0] // 2
+    tok = normed_ref.shape[0]
+    half = tok // 2
+    deep = count // 4
+    level = me // 4
+    line_rows = deep * tok
+    two_heads = 2 * HEAD_SIZE
+    flip_one = me + 1 - 2 * lax.rem(me, 2)
+    flip_two = me + 2 - 4 * lax.rem(me // 2, 2)
+    flip_both = flip_one + flip_two - me
+    near = (flip_two, flip_one)
+    far = (flip_one, flip_two)
+    greet_all(count)
+
+    def place(owner):
+        return (lax.rem(owner, 4) * deep + owner // 4) * tok
+
+    def piece(part, owner):
+        return held.at[pl.ds(pl.multiple_of(place(owner) + part * half, half), half), :]
+
+    def hop(part, owner, way):
+        to = (me + 4, me - 4, near[part], far[part])[way]
+        return pltpu.make_async_remote_copy(
+            src_ref=piece(part, owner),
+            dst_ref=piece(part, owner),
+            send_sem=hop_send.at[part, way, owner],
+            recv_sem=hop_recv.at[part, owner],
+            device_id=(to, core),
+            device_id_type=MESH,
+        )
+
+    def came(part, owner):
+        pltpu.make_async_remote_copy(
+            src_ref=piece(part, owner),
+            dst_ref=piece(part, owner),
+            send_sem=hop_send.at[part, 0, owner],
+            recv_sem=hop_recv.at[part, owner],
+            device_id=(flip_one, core),
+            device_id_type=MESH,
+        ).wait_recv()
+
+    def on_line(part, away_by, act, wait):
+        for up in (True, False):
+            owner = me - 4 * away_by if up else me + 4 * away_by
+            there = level >= away_by if up else level + away_by < deep
+            onward = level < deep - 1 if up else level > 0
+
+            @pl.when(there)
+            def _():
+                if wait:
+                    came(part, owner)
+
+                @pl.when(onward)
+                def _():
+                    act(hop(part, owner, 0 if up else 1))
+
+                if away_by > 0 or up:
+                    act(hop(part, owner, 2))
+                    act(hop(part, owner, 3))
+
+    def on_next(part, away_by, act, wait):
+        for up in (True, False):
+            if away_by == 0 and not up:
+                continue
+            owner = near[part] - 4 * away_by if up else near[part] + 4 * away_by
+            there = level >= away_by if up else level + away_by < deep
+
+            @pl.when(there)
+            def _():
+                if wait:
+                    came(part, owner)
+                act(hop(part, owner, 3))
+
+    def begin(copy):
+        copy.start()
+
+    held[pl.ds(pl.multiple_of(place(me), tok), tok), :] = normed_ref[...]
+    for away_by in range(deep + 1):
+        for part in range(2):
+            if away_by < deep:
+                on_line(part, away_by, begin, away_by > 0)
+        for part in range(2):
+            if away_by > 0:
+                on_next(part, away_by - 1, begin, True)
+
+    def core_copy(number):
+        rows = pl.ds(number * line_rows, line_rows)
+        return pltpu.make_async_remote_copy(
+            src_ref=away.at[rows, :],
+            dst_ref=arrived.at[rows, :],
+            send_sem=core_send.at[number],
+            recv_sem=core_recv.at[number],
+            device_id=(me, 1 - core),
+            device_id_type=MESH,
+        )
+
+    chunk = 256
+
+    def multiply(number, lead):
+        source = lax.rem(lead, 4) * line_rows
+
+        def one(index, carry):
+            block = held[pl.ds(pl.multiple_of(source + index * chunk, chunk), chunk), :]
+            product = jnp.dot(block, weight_ref[...], preferred_element_type=jnp.float32)
+            rows = pl.ds(pl.multiple_of(number * line_rows + index * chunk, chunk), chunk)
+            kept[rows, :] = product[:, :two_heads]
+            away[rows, :] = product[:, two_heads:]
+            return carry
+
+        lax.fori_loop(0, line_rows // chunk, one, 0)
+        core_copy(number).start()
+
+    which = lax.rem(me, 2)
+
+    def token_rows(owner):
+        return pl.ds(pl.multiple_of(owner * tok, tok), tok)
+
+    def pair_copy(owner):
+        return pltpu.make_async_remote_copy(
+            src_ref=pair_all.at[which, token_rows(owner), :],
+            dst_ref=pair_all.at[which, token_rows(owner), :],
+            send_sem=pair_send.at[owner],
+            recv_sem=pair_recv.at[owner],
+            device_id=(flip_one, core),
+            device_id_type=MESH,
+        )
+
+    def pair_came(owner):
+        view = pair_all.at[1 - which, token_rows(owner), :]
+        pltpu.make_async_remote_copy(
+            src_ref=view,
+            dst_ref=view,
+            send_sem=pair_send.at[owner],
+            recv_sem=pair_recv.at[owner],
+            device_id=(flip_one, core),
+            device_id_type=MESH,
+        ).wait_recv()
+
+    def settle(number, lead):
+        core_copy(number).wait()
+
+        def one(index, carry):
+            owner = index * 4 + lax.rem(lead, 4)
+            rows = pl.ds(pl.multiple_of(number * line_rows + index * tok, tok), tok)
+            total = kept[rows, :] + arrived[rows, :]
+            cosine = cosine_ref[token_rows(owner), :]
+            sine = sine_ref[token_rows(owner), :]
+            query = total[:, :HEAD_SIZE]
+            other = total[:, HEAD_SIZE:]
+            query_all[token_rows(owner), :] = (
+                query * cosine + pltpu.roll(query, HEAD_SIZE // 2, 1) * sine
+            ).astype(jnp.bfloat16)
+            turned = other * cosine + pltpu.roll(other, HEAD_SIZE // 2, 1) * sine
+            pair_all[which, token_rows(owner), :] = jnp.where(which == 0, turned, other).astype(
+                jnp.bfloat16
+            )
+            pair_copy(owner).start()
+            return carry
+
+        lax.fori_loop(0, deep, one, 0)
+
+    def line_came(part, lead):
+        def one(index, carry):
+            came(part, index * 4 + lax.rem(lead, 4))
+            return carry
+
+        lax.fori_loop(0, deep, one, 0)
+
+    multiply(0, me)
+    line_came(1, flip_two)
+    multiply(1, flip_two)
+    settle(0, me)
+    line_came(0, flip_one)
+    multiply(2, flip_one)
+    settle(1, flip_two)
+    settle(2, flip_one)
+    line_came(0, flip_both)
+    line_came(1, flip_both)
+    multiply(3, flip_both)
+    settle(3, flip_both)
+
+    def pair_done(owner, carry):
+        pair_copy(owner).wait_send()
+        pair_came(owner)
+        return carry
+
+    lax.fori_loop(0, count, pair_done, 0)
+
     blocks = 2 * count
-    greet_all(count)
     own_columns = pl.ds(pl.multiple_of(me * HEAD_SIZE, HEAD_SIZE), HEAD_SIZE)
 
     def home(block):
@@ -646,7 +854,9 @@
     per_tile = QUERY_TILE // half
 
     def one_tile(tile, carry):
-        attend_tile(tile, band, query_ref, key_ref, value_ref, low_ref, mixed)
+        attend_tile(
+            tile, band, query_all, pair_all.at[0], pair_all.at[1], low_ref, mixed
+        )
         for part in range(per_tile):
             block = tile * per_tile + part
             to, odd = home(block)
@@ -663,6 +873,14 @@
 
     lax.fori_loop(0, blocks // per_tile, one_tile, 0)
 
+    def sent(copy):
+        copy.wait_send()
+
+    for away_by in range(deep):
+        for part in range(2):
+            on_line(part, away_by, sent, False)
+            on_next(part, away_by, sent, False)
+
     def finish(block, carry):
         to, odd = home(block)
 
@@ -678,7 +896,7 @@
 
     lax.fori_loop(0, blocks, finish, 0)
 
-    def arrived(step, carry):
+    def landed(step, carry):
         sender = lax.rem(me + step, count)
         left = pl.multiple_of(sender * HEAD_SIZE, HEAD_SIZE)
         for odd in range(2):
@@ -693,29 +911,54 @@
             ).wait_recv()
         return carry
 
-    lax.fori_loop(1, count, arrived, 0)
-
-
-def second_attention(count, band, queries, keys, values, low):
-    tokens = queries.shape[0]
+    lax.fori_loop(1, count, landed, 0)
+
+
+def second_layer(count, band, normed, weights, cosine, sine, low):
+    tok, width = normed.shape
+    tokens = tok * count
     dma = pltpu.SemaphoreType.DMA
     vmem = pl.BlockSpec(memory_space=pltpu.VMEM)
+    wide = pltpu.VMEM((tokens, 2 * HEAD_SIZE), jnp.float32)
     return pl.pallas_call(
         partial(second_kernel, count, band),
-        out_shape=jax.ShapeDtypeStruct((tokens // count, count * HEAD_SIZE), jnp.bfloat16),
-        in_specs=[vmem] * 4,
+        out_shape=jax.ShapeDtypeStruct((tok, count * HEAD_SIZE), jnp.bfloat16),
+        in_specs=[vmem] * 5,
         out_specs=pl.BlockSpec(memory_space=pl.ANY),
         scratch_shapes=[
+            pltpu.VMEM((tokens, width), jnp.bfloat16),
+            wide,
+            wide,
+            wide,
             pltpu.VMEM((tokens, HEAD_SIZE), jnp.bfloat16),
+            pltpu.VMEM((2, tokens, HEAD_SIZE), jnp.bfloat16),
+            pltpu.VMEM((tokens, HEAD_SIZE), jnp.bfloat16),
+            dma((2, 4, count)),
+            dma((2, count)),
+            dma((4,)),
+            dma((4,)),
+            dma((count,)),
+            dma((count,)),
             dma((2 * count,)),
             dma((2, count)),
             dma((2,)),
         ],
         compiler_params=pltpu.CompilerParams(
-            collective_id=1, has_side_effects=True, vmem_limit_bytes=48 * 1024 * 1024
+            collective_id=1, has_side_effects=True, vmem_limit_bytes=56 * 1024 * 1024
         ),
-        name="second_attention",
-    )(queries, keys, values, low)
+        name="second_layer",
+    )(normed, weights, cosine, sine, low)
+
+
+def rotary_tables(positions):
+    half_dim = HEAD_SIZE // 2
+    speeds = THETA ** (-(jnp.arange(half_dim, dtype=jnp.float32) * 2.0 / HEAD_SIZE))
+    angles = (positions.astype(jnp.float32) * POSITION_FACTOR)[:, None] * speeds[None, :]
+    cosine, sine = jnp.cos(angles), jnp.sin(angles)
+    return (
+        jnp.concatenate([cosine, cosine], axis=1),
+        jnp.concatenate([-sine, sine], axis=1),
+    )
 
 
 def to_other_core(block):
@@ -776,20 +1019,9 @@
     factor = lax.rsqrt(jnp.mean(widened * widened, axis=1, keepdims=True) + EPS)
     gain_slice = lax.dynamic_slice_in_dim(pre_gain, core * col_width, col_width, 0)
     normed = (gain_slice[None, :] * resid_out.astype(jnp.float32) * factor).astype(jnp.bfloat16)
-    gathered = lax.all_gather(normed, "ctx", axis=0, tiled=True)
-    away = jnp.dot(gathered, weights[:, 2 * HEAD_SIZE :], preferred_element_type=jnp.float32)
-    arrived = to_other_core(away)
-    kept = jnp.dot(gathered, weights[:, : 2 * HEAD_SIZE], preferred_element_type=jnp.float32)
-    product = (kept + arrived).reshape(tokens, 2, HEAD_SIZE)
-    rotated = apply_rotary(product, positions, POSITION_FACTOR).astype(jnp.bfloat16)
-    even = lax.rem(me, 2) == 0
-    query_two = rotated[:, 0]
-    mine = jnp.where(even, rotated[:, 1], product[:, 1].astype(jnp.bfloat16))
-    theirs = from_partner(mine, "ctx", 0)
-    key_two = jnp.where(even, mine, theirs)
-    value_two = jnp.where(even, theirs, mine)
-    attended = second_attention(
-        count, tokens // 2, query_two, key_two, value_two, document[:, None]
+    cosine, sine = rotary_tables(positions)
+    attended = second_layer(
+        count, tokens // 2, normed, weights, cosine, sine, document[:, None]
     )
     return (resid_out, attended)
 

time: 378 us -> 291 us (0.77)
  waiting for transfers between devices: 169 us -> 0.01 us
  Pallas kernels: 135 us -> 256 us
  matrix products: 27 us -> 10.4 us
  between operations: 14.2 us -> 0.78 us
  local copies, waits for them, and re-layouts: 16.5 us -> 11.4 us
    all_gather x1 -> x0, waiting for transfers between devices: 153 us -> none  [shards_by_head(): gathered = lax.all_gather(normed, 'ctx', axis=0, tiled=True)]
    pallas_call x1, Pallas kernels: 19.1 us -> 141 us  [second_layer(): pl.pallas_call(partial(second_kernel, count, band), out_shape=jax.ShapeDt...]
    dot_general x2 -> x0, matrix products: 16.6 us -> none  [the longest x1 8.67 us: shards_by_head(): jnp.dot(gathered, weights[:, 2 * HEAD_SIZE:], preferred_element_type=jnp....]
    ppermute x1 -> x0, waiting for transfers between devices: 12.5 us -> none  [from_partner(): return lax.ppermute(block, axis, route)]
    cos x1 -> x0, other arithmetic: 5.54 us -> none  [apply_rotary(): cosine = jnp.cos(angles)[:, None, :]]
    unnamed x26 -> x21, local copies, waits for them, and re-layouts: 12.4 us -> 8.38 us
  transfers between devices with their start and end apart: 5 -> 2, of which waited for: 3 -> 0; matrix products, arithmetic and copies ran while one was open for 2% -> 3% of each run, Pallas kernels for 0% -> 0%
where the time goes in v2:
time: 291 us
  Pallas kernels  256 us (88%)
  other arithmetic  11.6 us (4%)
  local copies, waits for them, and re-layouts  11.4 us (4%)
  matrix products  10.4 us (4%)
    pallas_call x1, Pallas kernels, second_layer(): pl.pallas_call(partial(second_kernel, count, band), out_shape=jax.ShapeDt...  141 us
    pallas_call x1, Pallas kernels, first_attention(): pl.pallas_call(partial(first_kernel, count, band), out_shape=(jax.ShapeDt...  115 us
    dot_general x1, matrix products, shards_by_head(): jnp.dot(attend_one, out_one, preferred_element_type=jnp.float32)  10.4 us
    unnamed x21, local copies, waits for them, and re-layouts  8.38 us
  transfers between devices with their start and end apart: 2, of which 0 were waited for; matrix products, arithmetic and copies ran while one was open for 3% of the time, Pallas kernels for 0%

profile of v2, /device:TPU:0, one launch (start us, length us, event | category | flops | bytes accessed | tf_op | source)
XLA Modules:
  0.0 291.0 jit_solution(3676303889281380914)
XLA Ops:
  0.6 1.2 dynamic_slice.10
  1.9 1.3 iota_subtract_fusion
  3.2 0.4 copy.14.low_ref
  3.6 0.0 copy-start
  3.6 1.3 copy-done
  4.9 1.1 copy-done.1
  6.0 1.1 copy-done.2
  7.1 1.0 copy-done.3
  8.2 0.9 copy-done.4
  9.1 0.9 copy-done.5
  10.1 115.5 %first_attention.1 = (bf16[128,2048]{1,0:T(8,128)(2,1)S(1)}, bf16[2688,512]{1,0:T(8,128)(2,1)}) custom-call(bf16[128,2048]{1,0:T(8,128)(2,1)S(1)} %copy-done.3, bf16[128,1024]{1,0:T(8,128)(2,1)S(1)} %copy-done.4, bf16[128,1024]{1,0:T(8,128)(2,1)S(1)} %copy-done.5, s32[2048,1]{1,0:T(8,128)S(1)} %copy.14.low_ref, bf16[336,2048]{1,0:T(8,128)(2,1)S(1)} %copy-done, ...), custom_call_target="tpu_custom_call" | custom-call | tf_op jit(solution)/shard_map/first_attention/pallas_call | solution.py:588
  125.6 0.0 copy-start.6
  125.6 0.0 copy-start.9
  125.6 0.0 copy-start.7
  125.6 10.4 %convolution_convert_fusion = bf16[128,5376]{1,0:T(8,128)(2,1)S(1)} fusion(bf16[128,2048]{1,0:T(8,128)(2,1)S(1)} %get-tuple-element.4, bf16[2048,5376]{1,0:T(8,128)(2,1)} %param.16), kind=kOutput, calls=%fused_computation | convolution fusion | flops 2819260416 | bytes 23920640 | tf_op jit(solution)/shard_map/dot_general | solution.py:1002
  135.9 0.1 collective-permute-start.1
  136.0 0.0 copy-done.6
  136.0 0.5 collective-permute-start
  136.5 1.4 copy.15.low_ref
  137.9 0.0 copy-done.9
  137.9 0.1 dynamic_slice.12
  138.0 0.0 copy-done.7
  138.0 3.7 %fusion = (f32[2048,64]{1,0:T(8,128)S(1)}, f32[2048,64]{1,0:T(8,128)S(1)}, f32[2048,64]{1,0:T(8,128)S(1)}) fusion(f32[64]{0:T(128)S(1)} %negate_power_fusion, f32[2048]{0:T(1024)S(1)} %convert_multiply_fusion), kind=kLoop, calls=%fused_computation.11 | loop fusion | flops 262144 | bytes 1581312 | tf_op jit(solution)/shard_map/neg | solution.py:960
  141.7 0.0 copy-start.8
  141.7 1.9 pad_maximum_fusion
  143.7 0.0 collective-permute-done.1
  143.7 0.5 multiply_reduce_fusion.1
  144.3 0.0 collective-permute-done
  144.3 2.7 multiply_reduce_fusion
  147.0 1.3 multiply_convert_fusion
  148.3 140.8 %second_layer.1 = bf16[128,2048]{1,0:T(8,128)(2,1)} custom-call(bf16[128,2688]{1,0:T(8,128)(2,1)} %get-tuple-element.6.normed_ref, bf16[2688,512]{1,0:T(8,128)(2,1)} %get-tuple-element.5.weight_ref, f32[2048,128]{1,0:T(8,128)} %get-tuple-element.15.cosine_ref, f32[2048,128]{1,0:T(8,128)} %get-tuple-element.16.sine_ref, s32[2048,1]{1,0:T(8,128)} %copy.15.low_ref), custom_call_target="tpu_custom_call" | custom-call | tf_op jit(solution)/shard_map/second_layer/pallas_call | solution.py:923
  289.1 1.9 copy.17
  (10 shorter events, 0.0 us)
Async XLA Ops:
  3.6 1.3 copy-start
  4.9 1.1 copy-start.1
  6.0 1.1 copy-start.2
  7.1 1.0 copy-start.3
  8.2 0.9 copy-start.4
  9.1 0.9 copy-start.5
  125.6 10.5 %copy-start.6 = (bf16[128,2688]{1,0:T(8,128)(2,1)S(1)}, bf16[128,2688]{1,0:T(8,128)(2,1)}, u32[]{:S(2)}) copy-start(bf16[128,2688]{1,0:T(8,128)(2,1)} %param.12) | copy-start | bytes 2064388
  125.6 12.3 %copy-start.9 = (f32[5376]{0:T(1024)S(1)}, f32[5376]{0:T(1024)}, u32[]{:S(2)}) copy-start(f32[5376]{0:T(1024)} %param.18) | copy-start | bytes 64516
  125.6 12.4 %copy-start.7 = (s32[2048]{0:T(1024)S(1)}, s32[2048]{0:T(1024)}, u32[]{:S(2)}) copy-start(s32[2048]{0:T(1024)} %param.23) | copy-start | bytes 24580
  135.9 7.7 %collective-permute-start.1 = (bf16[128,5376]{1,0:T(8,128)(2,1)S(1)}, bf16[128,5376]{1,0:T(8,128)(2,1)S(1)}, u32[]{:S(2)}, u32[]{:S(2)}) collective-permute-start(bf16[128,5376]{1,0:T(8,128)(2,1)S(1)} %convolution_convert_fusion), channel_id=1, source_target_pairs={{0,1},{1,0},{2,3},{3,2},{4,5},{5,4},{6,7},{7,6},{8,9},{9,8},{10,11... | collective-permute-start | bytes 4128776 | tf_op jit(solution)/shard_map/ppermute | solution.py:965
  136.0 8.2 %collective-permute-start = (bf16[128,2688]{1,0:T(8,128)(2,1)S(1)}, bf16[128,2688]{1,0:T(8,128)(2,1)}, u32[]{:S(2)}, u32[]{:S(2)}) collective-permute-start(bf16[128,2688]{1,0:T(8,128)(2,1)S(1)} %copy-done.6), channel_id=1, source_target_pairs={{0,1},{1,0},{2,3},{3,2},{4,5},{5,4},{6,7},{7,6},{8,9},{9,8},{10,11... | collective-permute-start | bytes 2064392 | tf_op jit(solution)/shard_map/ppermute | solution.py:965
  141.7 2.5 copy-start.8

commit v3 on v2

--- a/solution.py
+++ b/solution.py
@@ -310,6 +310,10 @@
 QUERY_TILE = 256
 
 
+def early_rows(depth):
+    return depth * 2 // 7 // 16 * 16
+
+
 def spread_fits(mesh):
     return mesh.shape["heads"] == 2 and mesh.shape["ctx"] == 16
 
@@ -358,6 +362,98 @@
         preferred_element_type=jnp.float32,
     )
     mixed_ref[pl.ds(first, QUERY_TILE), :] = (mixed / total).astype(jnp.bfloat16)
+
+
+def weight_spread(count, sources, target, first, size, stride, offset, w_send, w_recv, w_own):
+    me, core = lax.axis_index("ctx"), lax.axis_index("heads")
+    half = count // 2
+    to_core = me // half
+    place = lax.rem(me, half)
+    apart = jnp.where(to_core == core, 0, 1)
+    wq_ref, wk_ref, wv_ref = sources
+
+    def spot(from_place, slot):
+        top = pl.multiple_of(from_place * stride + offset, 16)
+        left = pl.multiple_of(slot * HEAD_SIZE, HEAD_SIZE)
+        return target.at[pl.ds(top, size), pl.ds(left, HEAD_SIZE)]
+
+    def block(ref, index):
+        left = pl.multiple_of(index * HEAD_SIZE, HEAD_SIZE)
+        return ref.at[pl.ds(first, size), pl.ds(left, HEAD_SIZE)]
+
+    def views(pair, odd):
+        second = wk_ref if odd == 0 else wv_ref
+        return (
+            (block(wq_ref, 2 * pair + odd), spot(place, apart * 2)),
+            (block(second, pair), spot(place, apart * 2 + 1)),
+        )
+
+    def remote(pair, odd):
+        to = 2 * pair + odd
+        return [
+            pltpu.make_async_remote_copy(
+                src_ref=source,
+                dst_ref=landing,
+                send_sem=w_send.at[kind, to],
+                recv_sem=w_recv.at[kind, place * 2 + apart],
+                device_id=(to, to_core),
+                device_id_type=MESH,
+            )
+            for kind, (source, landing) in enumerate(views(pair, odd))
+        ]
+
+    def local(pair, odd):
+        return [
+            pltpu.make_async_copy(source, landing, w_own.at[kind])
+            for kind, (source, landing) in enumerate(views(pair, odd))
+        ]
+
+    def each(low, high, act_remote, act_local):
+        def body(pair, carry):
+            for odd in range(2):
+                mine = (2 * pair + odd == me) & (to_core == core)
+
+                @pl.when(jnp.logical_not(mine))
+                def _():
+                    for copy in remote(pair, odd):
+                        act_remote(copy)
+
+                @pl.when(mine)
+                def _():
+                    for copy in local(pair, odd):
+                        act_local(copy)
+
+            return carry
+
+        lax.fori_loop(low, high, body, 0)
+
+    def one_arrived(slot, carry):
+        from_place, from_apart = slot // 2, lax.rem(slot, 2)
+        mine = (core * half + from_place == me) & (from_apart == 0)
+
+        @pl.when(jnp.logical_not(mine))
+        def _():
+            for kind in range(2):
+                view = spot(from_place, from_apart * 2 + kind)
+                pltpu.make_async_remote_copy(
+                    src_ref=view,
+                    dst_ref=view,
+                    send_sem=w_send.at[kind, 0],
+                    recv_sem=w_recv.at[kind, slot],
+                    device_id=(me, 1 - core),
+                    device_id_type=MESH,
+                ).wait_recv()
+
+        return carry
+
+    def start(low, high):
+        each(low, high, lambda copy: copy.start(), lambda copy: copy.start())
+
+    def finish():
+        each(0, half, lambda copy: copy.wait_send(), lambda copy: copy.wait())
+        lax.fori_loop(0, count, one_arrived, 0)
+
+    return start, finish
 
 
 def first_kernel(
@@ -388,8 +484,8 @@
 ):
     me, core = lax.axis_index("ctx"), lax.axis_index("heads")
     tok = query_in.shape[0]
-    depth = wq_ref.shape[0]
     half = count // 2
+    early = weight_out.shape[0] // half
     greet_all(count)
 
     def columns(index):
@@ -444,64 +540,10 @@
         copy.wait()
     lax.fori_loop(1, count, wait_inward, 0)
 
-    to_core = me // half
-    place = lax.rem(me, half)
-    apart = jnp.where(to_core == core, 0, 1)
-
-    def weight_views(pair, odd):
-        to = 2 * pair + odd
-        base = pl.multiple_of(apart * 2 * HEAD_SIZE, HEAD_SIZE)
-        next_base = pl.multiple_of(apart * 2 * HEAD_SIZE + HEAD_SIZE, HEAD_SIZE)
-        second = wk_ref if odd == 0 else wv_ref
-        return (
-            (wq_ref.at[:, columns(to)], weight_out.at[rows(place, depth), pl.ds(base, HEAD_SIZE)]),
-            (
-                second.at[:, columns(pair)],
-                weight_out.at[rows(place, depth), pl.ds(next_base, HEAD_SIZE)],
-            ),
-        )
-
-    def weight_remote(pair, odd):
-        to = 2 * pair + odd
-        return [
-            pltpu.make_async_remote_copy(
-                src_ref=source,
-                dst_ref=target,
-                send_sem=w_send.at[kind, to],
-                recv_sem=w_recv.at[kind, place * 2 + apart],
-                device_id=(to, to_core),
-                device_id_type=MESH,
-            )
-            for kind, (source, target) in enumerate(weight_views(pair, odd))
-        ]
-
-    def weight_local(pair, odd):
-        return [
-            pltpu.make_async_copy(source, target, w_own.at[kind])
-            for kind, (source, target) in enumerate(weight_views(pair, odd))
-        ]
-
-    def each_weight(act_remote, act_local):
-        def body(pair, carry):
-            for odd in range(2):
-                to = 2 * pair + odd
-                mine = (to == me) & (to_core == core)
-
-                @pl.when(jnp.logical_not(mine))
-                def _():
-                    for copy in weight_remote(pair, odd):
-                        act_remote(copy)
-
-                @pl.when(mine)
-                def _():
-                    for copy in weight_local(pair, odd):
-                        act_local(copy)
-
-            return carry
-
-        lax.fori_loop(0, half, body, 0)
-
-    each_weight(lambda copy: copy.start(), lambda copy: copy.start())
+    weight_start, weight_finish = weight_spread(
+        count, (wq_ref, wk_ref, wv_ref), weight_out, 0, early, early, 0, w_send, w_recv, w_own
+    )
+    weight_start(0, half)
 
     def outward(to):
         return pltpu.make_async_remote_copy(
@@ -552,33 +594,10 @@
 
     lax.fori_loop(1, count, finish, 0)
     outward_own().wait()
-    each_weight(lambda copy: copy.wait_send(), lambda copy: copy.wait())
-
-    def weight_arrived(slot, carry):
-        from_place, from_apart = slot // 2, lax.rem(slot, 2)
-        sender = core * half + from_place
-        mine = (sender == me) & (from_apart == 0)
-
-        @pl.when(jnp.logical_not(mine))
-        def _():
-            for kind in range(2):
-                left = pl.multiple_of((from_apart * 2 + kind) * HEAD_SIZE, HEAD_SIZE)
-                view = weight_out.at[rows(from_place, depth), pl.ds(left, HEAD_SIZE)]
-                pltpu.make_async_remote_copy(
-                    src_ref=view,
-                    dst_ref=view,
-                    send_sem=w_send.at[kind, 0],
-                    recv_sem=w_recv.at[kind, slot],
-                    device_id=(me, 1 - core),
-                    device_id_type=MESH,
-                ).wait_recv()
-
-        return carry
-
-    lax.fori_loop(0, count, weight_arrived, 0)
-
-
-def first_attention(count, band, queries, keys, values, low, wq, wk, wv):
+    weight_finish()
+
+
+def first_attention(count, band, early, queries, keys, values, low, wq, wk, wv):
     tok = queries.shape[0]
     tokens = tok * count
     whole = (tokens, HEAD_SIZE)
@@ -589,9 +608,9 @@
         partial(first_kernel, count, band),
         out_shape=(
             jax.ShapeDtypeStruct(queries.shape, jnp.bfloat16),
-            jax.ShapeDtypeStruct((wq.shape[0] * count // 2, 4 * HEAD_SIZE), jnp.bfloat16),
+            jax.ShapeDtypeStruct((early * count // 2, 4 * HEAD_SIZE), jnp.bfloat16),
         ),
-        in_specs=[vmem] * 4 + [anywhere] * 3,
+        in_specs=[anywhere] * 3 + [vmem] + [anywhere] * 3,
         out_specs=(anywhere, anywhere),
         scratch_shapes=[pltpu.VMEM(whole, jnp.bfloat16)] * 4
         + [
@@ -616,11 +635,15 @@
     count,
     band,
     normed_ref,
-    weight_ref,
+    early_ref,
+    wq_ref,
+    wk_ref,
+    wv_ref,
     cosine_ref,
     sine_ref,
     low_ref,
     attend_out,
+    weight_ref,
     held,
     kept,
     away,
@@ -637,6 +660,10 @@
     back_send,
     back_recv,
     back_own,
+    w_send,
+    w_recv,
+    w_own,
+    early_sem,
 ):
     me, core = lax.axis_index("ctx"), lax.axis_index("heads")
     tok = normed_ref.shape[0]
@@ -715,6 +742,30 @@
         copy.start()
 
     held[pl.ds(pl.multiple_of(place(me), tok), tok), :] = normed_ref[...]
+    depth = wq_ref.shape[0]
+    places = count // 2
+    early = early_ref.shape[0] // places
+    weight_start, weight_finish = weight_spread(
+        count,
+        (wq_ref, wk_ref, wv_ref),
+        weight_ref,
+        early,
+        depth - early,
+        depth,
+        early,
+        w_send,
+        w_recv,
+        w_own,
+    )
+    batch = places // deep
+    moved = [
+        pltpu.make_async_copy(
+            early_ref.at[pl.ds(index * early, early), :],
+            weight_ref.at[pl.ds(index * depth, early), :],
+            early_sem.at[index],
+        )
+        for index in range(places)
+    ]
     for away_by in range(deep + 1):
         for part in range(2):
             if away_by < deep:
@@ -722,6 +773,11 @@
         for part in range(2):
             if away_by > 0:
                 on_next(part, away_by - 1, begin, True)
+        if away_by < deep:
+            weight_start(away_by * batch, (away_by + 1) * batch)
+        if away_by == 0:
+            for copy in moved:
+                copy.start()
 
     def core_copy(number):
         rows = pl.ds(number * line_rows, line_rows)
@@ -806,6 +862,9 @@
 
         lax.fori_loop(0, deep, one, 0)
 
+    for copy in moved:
+        copy.wait()
+    weight_finish()
     multiply(0, me)
     line_came(1, flip_two)
     multiply(1, flip_two)
@@ -914,18 +973,20 @@
     lax.fori_loop(1, count, landed, 0)
 
 
-def second_layer(count, band, normed, weights, cosine, sine, low):
+def second_layer(count, band, normed, weights, wq, wk, wv, cosine, sine, low):
     tok, width = normed.shape
     tokens = tok * count
     dma = pltpu.SemaphoreType.DMA
     vmem = pl.BlockSpec(memory_space=pltpu.VMEM)
+    anywhere = pl.BlockSpec(memory_space=pl.ANY)
     wide = pltpu.VMEM((tokens, 2 * HEAD_SIZE), jnp.float32)
     return pl.pallas_call(
         partial(second_kernel, count, band),
         out_shape=jax.ShapeDtypeStruct((tok, count * HEAD_SIZE), jnp.bfloat16),
-        in_specs=[vmem] * 5,
-        out_specs=pl.BlockSpec(memory_space=pl.ANY),
+        in_specs=[vmem] + [anywhere] * 4 + [vmem] * 3,
+        out_specs=anywhere,
         scratch_shapes=[
+            pltpu.VMEM((wq.shape[0] * count // 2, 4 * HEAD_SIZE), jnp.bfloat16),
             pltpu.VMEM((tokens, width), jnp.bfloat16),
             wide,
             wide,
@@ -942,12 +1003,16 @@
             dma((2 * count,)),
             dma((2, count)),
             dma((2,)),
+            dma((2, count)),
+            dma((2, count)),
+            dma((2,)),
+            dma((count // 2,)),
         ],
         compiler_params=pltpu.CompilerParams(
             collective_id=1, has_side_effects=True, vmem_limit_bytes=56 * 1024 * 1024
         ),
         name="second_layer",
-    )(normed, weights, cosine, sine, low)
+    )(normed, weights, wq, wk, wv, cosine, sine, low)
 
 
 def rotary_tables(positions):
@@ -988,9 +1053,11 @@
     own_window = lax.dynamic_index_in_dim(window, me, 0, keepdims=False)
     low_one = jnp.maximum(document, token - own_window + 1)
     resid_other = to_other_core(resid_in)
+    early = early_rows(proj_query.shape[0])
     attend_one, weights = first_attention(
         count,
         LONGEST_WINDOW,
+        early,
         first_layer_queries,
         first_layer_keys,
         first_layer_values,
@@ -1021,7 +1088,16 @@
     normed = (gain_slice[None, :] * resid_out.astype(jnp.float32) * factor).astype(jnp.bfloat16)
     cosine, sine = rotary_tables(positions)
     attended = second_layer(
-        count, tokens // 2, normed, weights, cosine, sine, document[:, None]
+        count,
+        tokens // 2,
+        normed,
+        weights,
+        proj_query,
+        key_projection,
+        value_projection,
+        cosine,
+        sine,
+        document[:, None],
     )
     return (resid_out, attended)
 

time: 291 us -> 270 us (0.928)
  Pallas kernels: 256 us -> 234 us
    pallas_call x1, Pallas kernels: 115 us -> 76.6 us  [first_attention(): pl.pallas_call(partial(first_kernel, count, band), out_shape=(jax.ShapeDt...]
    pallas_call x1, Pallas kernels: 141 us -> 158 us  [second_layer(): pl.pallas_call(partial(second_kernel, count, band), out_shape=jax.ShapeDt...]
    unnamed x21 -> x23, local copies, waits for them, and re-layouts: 8.38 us -> 8.39 us
where the time goes in v3:
time: 270 us; the launch traced here: 269 us
  Pallas kernels  234 us (87%)
  other arithmetic  11.5 us (4%)
  local copies, waits for them, and re-layouts  11.4 us (4%)
  matrix products  10.6 us (4%)
    pallas_call x1, Pallas kernels, second_layer(): pl.pallas_call(partial(second_kernel, count, band), out_shape=jax.ShapeDt...  158 us
    pallas_call x1, Pallas kernels, first_attention(): pl.pallas_call(partial(first_kernel, count, band), out_shape=(jax.ShapeDt...  76.6 us
    dot_general x1, matrix products, shards_by_head(): jnp.dot(attend_one, out_one, preferred_element_type=jnp.float32)  10.6 us
    unnamed x23, local copies, waits for them, and re-layouts  8.39 us
  transfers between devices with their start and end apart: 2, of which 0 were waited for; matrix products, arithmetic and copies ran while one was open for 3% of the time, Pallas kernels for 0%

profile of v3, /device:TPU:0, one launch (start us, length us, event | category | flops | bytes accessed | tf_op | source)
XLA Modules:
  0.0 269.0 jit_solution(2818593441208358123)
XLA Ops:
  0.6 1.2 dynamic_slice.10
  1.9 1.3 iota_subtract_fusion
  3.2 0.4 copy.14.low_ref
  3.6 0.0 copy-start
  3.6 1.3 copy-done
  4.9 1.1 copy-done.1
  6.0 1.1 copy-done.2
  7.1 1.0 copy-done.4
  8.2 0.9 copy-done.5
  9.1 0.9 copy-done.6
  10.1 76.6 %first_attention.1 = (bf16[128,2048]{1,0:T(8,128)(2,1)S(1)}, bf16[768,512]{1,0:T(8,128)(2,1)S(1)}) custom-call(bf16[128,2048]{1,0:T(8,128)(2,1)S(1)} %copy-done.4, bf16[128,1024]{1,0:T(8,128)(2,1)S(1)} %copy-done.5, bf16[128,1024]{1,0:T(8,128)(2,1)S(1)} %copy-done.6, s32[2048,1]{1,0:T(8,128)S(1)} %copy.14.low_ref, bf16[336,2048]{1,0:T(8,128)(2,1)S(1)} %copy-done, ...), custom_call_target="tpu_custom_call" | custom-call | tf_op jit(solution)/shard_map/first_attention/pallas_call | solution.py:607
  86.7 0.0 copy-start.3
  86.7 0.0 copy-start.7
  86.7 0.0 copy-start.10
  86.7 0.0 copy-start.8
  86.7 10.6 %convolution_convert_fusion = bf16[128,5376]{1,0:T(8,128)(2,1)S(1)} fusion(bf16[128,2048]{1,0:T(8,128)(2,1)S(1)} %get-tuple-element.4, bf16[2048,5376]{1,0:T(8,128)(2,1)} %param.16), kind=kOutput, calls=%fused_computation | convolution fusion | flops 2819260416 | bytes 23920640 | tf_op jit(solution)/shard_map/dot_general | solution.py:1069
  97.3 0.1 collective-permute-start.1
  97.4 0.0 copy-done.7
  97.4 0.5 collective-permute-start
  97.9 1.3 copy.15.low_ref
  99.3 0.0 copy-done.10
  99.3 0.1 dynamic_slice.12
  99.4 3.7 %fusion = (f32[2048,64]{1,0:T(8,128)S(1)}, f32[2048,64]{1,0:T(8,128)S(1)}, f32[2048,64]{1,0:T(8,128)S(1)}) fusion(f32[64]{0:T(128)S(1)} %negate_power_fusion, f32[2048]{0:T(1024)S(1)} %convert_multiply_fusion), kind=kLoop, calls=%fused_computation.11 | loop fusion | flops 262144 | bytes 1581312 | tf_op jit(solution)/shard_map/neg | solution.py:1025
  103.1 0.0 copy-start.9
  103.1 1.9 pad_maximum_fusion
  105.0 0.0 collective-permute-done.1
  105.0 0.5 multiply_reduce_fusion.1
  105.6 0.0 collective-permute-done
  105.6 2.7 multiply_reduce_fusion
  108.3 1.3 multiply_convert_fusion
  109.6 157.5 %second_layer.1 = bf16[128,2048]{1,0:T(8,128)(2,1)} custom-call(bf16[128,2688]{1,0:T(8,128)(2,1)} %get-tuple-element.6.normed_ref, bf16[768,512]{1,0:T(8,128)(2,1)} %copy-done.3, bf16[336,2048]{1,0:T(8,128)(2,1)} %wq_ref.3, bf16[336,1024]{1,0:T(8,128)(2,1)} %wk_ref.3, bf16[336,1024]{1,0:T(8,128)(2,1)} %wv_ref.3, f32[2048,128]{1,0:T(8,128)} %get-tuple-element.15.cosine_ref, ...), custom_call_target="tpu_custom_call" | custom-call | tf_op jit(solution)/shard_map/second_layer/pallas_call | solution.py:983
  267.1 1.9 copy.17
  (12 shorter events, 0.0 us)
Async XLA Ops:
  3.6 1.3 copy-start
  4.9 1.1 copy-start.1
  6.0 1.1 copy-start.2
  7.1 1.0 copy-start.4
  8.2 0.9 copy-start.5
  9.1 0.9 copy-start.6
  86.7 10.7 %copy-start.3 = (bf16[768,512]{1,0:T(8,128)(2,1)}, bf16[768,512]{1,0:T(8,128)(2,1)S(1)}, u32[]{:S(2)}) copy-start(bf16[768,512]{1,0:T(8,128)(2,1)S(1)} %get-tuple-element.5.early_ref) | copy-start | bytes 2359300
  86.7 10.7 %copy-start.7 = (bf16[128,2688]{1,0:T(8,128)(2,1)S(1)}, bf16[128,2688]{1,0:T(8,128)(2,1)}, u32[]{:S(2)}) copy-start(bf16[128,2688]{1,0:T(8,128)(2,1)} %param.12) | copy-start | bytes 2064388
  86.7 12.6 %copy-start.10 = (f32[5376]{0:T(1024)S(1)}, f32[5376]{0:T(1024)}, u32[]{:S(2)}) copy-start(f32[5376]{0:T(1024)} %param.18) | copy-start | bytes 64516
  86.7 12.6 %copy-start.8 = (s32[2048]{0:T(1024)S(1)}, s32[2048]{0:T(1024)}, u32[]{:S(2)}) copy-start(s32[2048]{0:T(1024)} %param.23) | copy-start | bytes 24580
  97.3 7.7 %collective-permute-start.1 = (bf16[128,5376]{1,0:T(8,128)(2,1)S(1)}, bf16[128,5376]{1,0:T(8,128)(2,1)S(1)}, u32[]{:S(2)}, u32[]{:S(2)}) collective-permute-start(bf16[128,5376]{1,0:T(8,128)(2,1)S(1)} %convolution_convert_fusion), channel_id=1, source_target_pairs={{0,1},{1,0},{2,3},{3,2},{4,5},{5,4},{6,7},{7,6},{8,9},{9,8},{10,11... | collective-permute-start | bytes 4128776 | tf_op jit(solution)/shard_map/ppermute | solution.py:1030
  97.4 8.2 %collective-permute-start = (bf16[128,2688]{1,0:T(8,128)(2,1)S(1)}, bf16[128,2688]{1,0:T(8,128)(2,1)}, u32[]{:S(2)}, u32[]{:S(2)}) collective-permute-start(bf16[128,2688]{1,0:T(8,128)(2,1)S(1)} %copy-done.7), channel_id=1, source_target_pairs={{0,1},{1,0},{2,3},{3,2},{4,5},{5,4},{6,7},{7,6},{8,9},{9,8},{10,11... | collective-permute-start | bytes 2064392 | tf_op jit(solution)/shard_map/ppermute | solution.py:1030
  103.1 2.5 copy-start.9
